TPU v7x, 32 devices: a whole 2x2x4 slice. The times are simulated.
32 devices in a mesh: gx: 4 (over x, core), gy: 8 (over z, y).
Axes of the slice: x: 2, y: 2, z: 4, core: 2. Of those that a mesh axis runs over, the one named last changes fastest.
Arguments:
- model_state: float32 [16, 256, 528], P('gx', 'gy'), may hold values from -6 to 6
- hyper_coef: float32 [528], replicated, may hold values from 0.0001 to 0.001
- point_mass: float32 [16, 256], P('gx', 'gy'), may hold values from 0.5 to 2
- inverse_mass: float32 [16, 256], P('gx', 'gy'), may hold values from 0.2 to 0.8
- span_slot: int32 [16, 256], P('gx', 'gy'), may hold values from 0 to 511, as said below
- vert_diff: float32 [8, 48, 512], P('gy', None, 'gx'), may hold values from 0.05 to 20
- fall_rate: float32 [8, 48, 512], P('gy', None, 'gx'), may hold values from 0.1 to 10
- cloud_frac: float32 [8, 48, 512], P('gy', None, 'gx'), may hold values from 0 to 1
Outputs:
- new_state: float32 [16, 256, 528], P('gx', 'gy')
Inputs may be any that keep to these rules, and one draw needn't show every extreme that they name: `span_slot`: within the columns that share a block of 32 along the second dimension, the values form a permutation; each device's 128 columns hold exactly 32 values in each range from p * 128 to (p + 1) * 128 - 1.
All inputs are finite; a program needn't handle non-finite values.
Results may differ from a plain program's by a relative error of at most 0.0003.
Values sent between devices are 32-bit elements; how exact they have to be, the bound alone decides.
No kernel may reach another device: no remote copies, remote signals or barrier semaphores. Data moves between devices by JAX's collectives and lax.ppermute only.
A program may use at most 64 MiB of HBM per device.

v0:
```python
import jax
import jax.numpy as jnp
import numpy as np
from jax import lax
from jax.sharding import PartitionSpec as P


def extended(block, sides, width):
    for axis, dim in sides:
        count = lax.axis_size(axis)
        forward = [(i, i + 1) for i in range(count - 1)]
        forward.append((count - 1, 0))
        backward = [(target, source) for source, target in forward]
        low = lax.ppermute(
            lax.slice_in_dim(block, block.shape[dim] - width, None, axis=dim), axis, forward
        )
        high = lax.ppermute(lax.slice_in_dim(block, 0, width, axis=dim), axis, backward)
        block = jnp.concatenate([low, block, high], axis=dim)
    return block


def second_table():
    nodes = np.array([-1.0, -1.0 / np.sqrt(5.0), 1.0 / np.sqrt(5.0), 1.0])
    deriv = np.zeros((4, 4))
    for row_index in range(4):
        for col_index in range(4):
            if row_index == col_index:
                deriv[row_index, col_index] = sum(
                    (
                        1.0 / (nodes[row_index] - nodes[other])
                        for other in range(4)
                        if other != row_index
                    )
                )
            else:
                upper_part = np.prod(
                    [nodes[row_index] - nodes[other] for other in range(4) if other != row_index]
                )
                lower_part = np.prod(
                    [nodes[col_index] - nodes[other] for other in range(4) if other != col_index]
                )
                deriv[row_index, col_index] = upper_part / (
                    lower_part * (nodes[row_index] - nodes[col_index])
                )
    return deriv @ deriv


def harmonic_operator(field):
    second_deriv = jnp.asarray(second_table(), jnp.float32)
    size_x, size_y, row_width = field.shape
    along_x = jnp.einsum(
        "ab,ebyf->eayf",
        second_deriv,
        field.reshape(size_x // 4, 4, size_y, row_width),
        precision=lax.Precision.HIGHEST,
    ).reshape(size_x, size_y, row_width)
    along_y = jnp.einsum(
        "ab,xebf->xeaf",
        second_deriv,
        field.reshape(size_x, size_y // 4, 4, row_width),
        precision=lax.Precision.HIGHEST,
    ).reshape(size_x, size_y, row_width)
    return along_x + along_y


def assemble(values, point_mass, inverse_mass):
    weighted = point_mass[:, :, None] * values
    size_x, size_y = point_mass.shape
    padded = extended(weighted, (("gx", 0), ("gy", 1)), 1)
    first_x = (jnp.arange(size_x) % 4 == 0)[:, None, None]
    last_x = (jnp.arange(size_x) % 4 == 3)[:, None, None]
    first_y = (jnp.arange(size_y) % 4 == 0)[None, :, None]
    last_y = (jnp.arange(size_y) % 4 == 3)[None, :, None]
    total = (
        weighted
        + jnp.where(first_x, padded[:-2, 1:-1], 0.0)
        + jnp.where(last_x, padded[2:, 1:-1], 0.0)
    )
    total = (
        total
        + jnp.where(first_y, padded[1:-1, :-2], 0.0)
        + jnp.where(last_y, padded[1:-1, 2:], 0.0)
    )
    total = total + jnp.where(first_x & first_y, padded[:-2, :-2], 0.0)
    total = total + jnp.where(first_x & last_y, padded[:-2, 2:], 0.0)
    total = total + jnp.where(last_x & first_y, padded[2:, :-2], 0.0)
    total = total + jnp.where(last_x & last_y, padded[2:, 2:], 0.0)
    return inverse_mass[:, :, None] * total


def physics(fields, diff_coef, fall_coef, overcast_fraction_weight):
    zero_row = jnp.zeros_like(diff_coef[:1])
    above = jnp.concatenate([zero_row, diff_coef[1:]], 0)
    below = jnp.concatenate([diff_coef[1:], zero_row], 0)
    surface = jnp.concatenate([jnp.zeros_like(diff_coef[1:]), diff_coef[:1]], 0)
    centre = 1.0 + above + below + surface

    def forward(state_carry, inputs):
        prev_gain, previous_value = state_carry
        sub_k, centre_k, sup_k, rhs_k = inputs
        divisor = centre_k - sub_k * prev_gain
        gain = sup_k / divisor
        value = (rhs_k + sub_k[None, :] * previous_value) / divisor[None, :]
        return ((gain, value), (gain, value))

    start = (jnp.zeros_like(diff_coef[0]), jnp.zeros_like(fields[0]))
    _, (gains, values) = lax.scan(forward, start, (above, centre, below, fields))

    def backward(next_solved, inputs):
        gain, value = inputs
        solved_line_entries = value + gain[None, :] * next_solved
        return (solved_line_entries, solved_line_entries)

    _, solved_line_entries = lax.scan(
        backward, jnp.zeros_like(fields[0]), (gains, values), reverse=True
    )
    thermal_state_kelvin = solved_line_entries[:, 0]
    humidity_mixing_ratio = solved_line_entries[:, 1]
    droplet_mixing_ratio = solved_line_entries[:, 2]
    condensed_mass_content = (
        overcast_fraction_weight
        * 0.5
        * jnp.maximum(humidity_mixing_ratio - 0.3 * thermal_state_kelvin, 0.0)
    )
    humidity_mixing_ratio = humidity_mixing_ratio - condensed_mass_content
    droplet_mixing_ratio = droplet_mixing_ratio + condensed_mass_content
    thermal_state_kelvin = thermal_state_kelvin + 2.0 * condensed_mass_content

    def settle(inflow, inputs):
        liquid_k, fall_k = inputs
        settled = (liquid_k + inflow) / (1.0 + fall_k)
        return (fall_k * settled, settled)

    _, droplet_mixing_ratio = lax.scan(
        settle, jnp.zeros_like(droplet_mixing_ratio[0]), (droplet_mixing_ratio, fall_coef)
    )
    return jnp.concatenate(
        [
            thermal_state_kelvin[:, None],
            humidity_mixing_ratio[:, None],
            droplet_mixing_ratio[:, None],
            solved_line_entries[:, 3:],
        ],
        1,
    )


def local(
    model_state, hyper_coef, point_mass, inverse_mass, span_slot, vert_diff, fall_rate, cloud_frac
):
    lap_once = assemble(harmonic_operator(model_state), point_mass, inverse_mass)
    lap_twice = assemble(harmonic_operator(lap_once), point_mass, inverse_mass)
    dynamic = model_state - hyper_coef[None, None, :] * lap_twice
    size_x, size_y, row_width = dynamic.shape
    levels = vert_diff.shape[1]
    variables = row_width // levels
    columns = size_x * size_y
    peers = lax.axis_size("gx")
    per_peer = columns // peers
    flat_state = dynamic.reshape(columns, row_width)
    position_labels = span_slot.reshape(columns)
    owner_order = jnp.argsort(position_labels // columns, stable=True)
    inverse_order = jnp.argsort(owner_order)
    sent_slots = position_labels[owner_order].reshape(peers, per_peer)
    local_diff = vert_diff[0]
    local_fall = fall_rate[0]
    local_cloud = cloud_frac[0]
    packed = flat_state[owner_order].reshape(peers, per_peer, row_width)
    arrived, arrived_slots = (
        lax.all_to_all(packed, "gx", split_axis=0, concat_axis=0, tiled=True),
        lax.all_to_all(sent_slots, "gx", split_axis=0, concat_axis=0, tiled=True),
    )
    local_slot = arrived_slots.reshape(columns) % columns
    fields = arrived.reshape(columns, variables, levels).transpose(2, 1, 0)
    updated = physics(
        fields,
        jnp.take(local_diff, local_slot, axis=1),
        jnp.take(local_fall, local_slot, axis=1),
        jnp.take(local_cloud, local_slot, axis=1),
    )
    tendency = (updated - fields).transpose(2, 1, 0).reshape(peers, per_peer, row_width)
    result_value = lax.all_to_all(tendency, "gx", split_axis=0, concat_axis=0, tiled=True)
    own_tendency = result_value.reshape(columns, row_width)[inverse_order]
    result = flat_state + own_tendency
    return result.reshape(size_x, size_y, row_width)


def solution(mesh):
    placed = (
        P("gx", "gy", None),
        P(),
        P("gx", "gy"),
        P("gx", "gy"),
        P("gx", "gy"),
        P("gy", None, "gx"),
        P("gy", None, "gx"),
        P("gy", None, "gx"),
    )
    return jax.shard_map(
        local, mesh=mesh, in_specs=placed, out_specs=P("gx", "gy", None), check_vma=False
    )
```

profile of v0, /device:TPU:0, one launch (start us, length us, event | category | flops | bytes accessed | tf_op | source)
XLA Modules:
  0.0 116.3 jit_solution(10063386367959736002)
XLA Ops:
  0.0 0.8 copy.93
  0.8 1.1 reshape.168
  2.8 0.7 copy-done
  3.5 0.8 fusion.12
  5.0 2.0 %collective-permute-start.1 = (f32[1,32,528]{2,0,1:T(1,128)S(1)}, f32[1,32,528]{2,0,1:T(1,128)S(1)}, u32[]{:S(2)}, u32[]{:S(2)}) collective-permute-start(f32[1,32,528]{2,0,1:T(1,128)S(1)} %get-tuple-element.377), channel_id=1, source_target_pairs={{8,0},{16,8},{24,16},{0,24},{9,1},{17,9},{25,17},{1,25},{10,2},{18... | collective-permute-start | bytes 202760 | tf_op jit(solution)/shard_map/ppermute | solution.py:17
  7.1 2.5 %sort.34 = (s32[128]{0:T(128)}, s32[128]{0:T(128)S(1)}) sort(s32[128]{0:T(128)S(1)} %and_select_fusion.1, s32[128]{0:T(128)S(1)} %iota.66), dimensions={0}, to_apply=%region_0.1 | sort | flops 896 | bytes 2048 | tf_op jit(solution)/shard_map/jit(argsort)/sort | solution.py:162
  9.6 1.2 %gather_fusion = s32[128]{0:T(128)S(1)} fusion(s32[128]{0:T(128)S(1)} %reshape.173, s32[1024]{0:T(1024)S(1)} %pad_clamp_fusion.2), kind=kCustom, calls=%fused_computation.3 | custom fusion | bytes 1536 | tf_op jit(solution)/shard_map/gather | solution.py:164
  11.5 3.5 %all-to-all-start = ((s32[4,1,32]{2,1,0:T(1,128)}), s32[4,1,32]{2,1,0:T(1,128)S(1)}, u32[]{:S(2)}, u32[]{:S(2)}) async-start(s32[4,1,32]{2,1,0:T(1,128)} %bitcast.12), calls=%async_computation | async-start | bytes 4096 | tf_op jit(solution)/shard_map/all_to_all | solution.py:171
  17.5 2.6 %sort.35 = (s32[128]{0:T(128)}, s32[128]{0:T(128)S(1)}) sort(s32[128]{0:T(128)S(1)} %get-tuple-element.186, s32[128]{0:T(128)S(1)} %iota.67), dimensions={0}, to_apply=%region_7.9 | sort | flops 896 | bytes 2048 | tf_op jit(solution)/shard_map/jit(argsort)/sort | solution.py:163
  21.5 2.1 %collective-permute-start.2 = (f32[6,1,528]{2,0,1:T(8,128)S(1)}, f32[6,1,528]{2,0,1:T(8,128)S(1)}, u32[]{:S(2)}, u32[]{:S(2)}) collective-permute-start(f32[6,1,528]{2,0,1:T(8,128)S(1)} %get-tuple-element.372), channel_id=1, source_target_pairs={{0,1},{1,2},{2,3},{3,4},{4,5},{5,6},{6,7},{7,0},{8,9},{9,10},{10,1... | collective-permute-start | bytes 38024 | tf_op jit(solution)/shard_map/ppermute | solution.py:14
  23.5 3.1 %collective-permute-start.3 = (f32[6,1,528]{2,0,1:T(8,128)S(1)}, f32[6,1,528]{2,0,1:T(8,128)S(1)}, u32[]{:S(2)}, u32[]{:S(2)}) collective-permute-start(f32[6,1,528]{2,0,1:T(8,128)S(1)} %get-tuple-element.373), channel_id=1, source_target_pairs={{1,0},{2,1},{3,2},{4,3},{5,4},{6,5},{7,6},{0,7},{9,8},{10,9},{11,1... | collective-permute-start | bytes 38024 | tf_op jit(solution)/shard_map/ppermute | solution.py:17
  26.6 1.7 %collective-permute-done.2 = f32[6,1,528]{2,0,1:T(8,128)S(1)} collective-permute-done((f32[6,1,528]{2,0,1:T(8,128)S(1)}, f32[6,1,528]{2,0,1:T(8,128)S(1)}, u32[]{:S(2)}, u32[]{:S(2)}) %collective-permute-start.2) | collective-permute-done | bytes 12704 | tf_op jit(solution)/shard_map/ppermute | solution.py:14
  28.6 1.0 fusion.28
  31.4 1.7 %collective-permute-start.5 = (f32[1,32,528]{2,0,1:T(1,128)S(1)}, f32[1,32,528]{2,0,1:T(1,128)S(1)}, u32[]{:S(2)}, u32[]{:S(2)}) collective-permute-start(f32[1,32,528]{2,0,1:T(1,128)S(1)} %get-tuple-element.375), channel_id=1, source_target_pairs={{8,0},{16,8},{24,16},{0,24},{9,1},{17,9},{25,17},{1,25},{10,2},{18... | collective-permute-start | bytes 202760 | tf_op jit(solution)/shard_map/ppermute | solution.py:17
  34.5 0.8 collective-permute-done.4
  35.7 1.4 %collective-permute-start.6 = (f32[6,1,528]{2,0,1:T(8,128)S(1)}, f32[6,1,528]{2,0,1:T(8,128)S(1)}, u32[]{:S(2)}, u32[]{:S(2)}) collective-permute-start(f32[6,1,528]{2,0,1:T(8,128)S(1)} %get-tuple-element.368), channel_id=1, source_target_pairs={{0,1},{1,2},{2,3},{3,4},{4,5},{5,6},{6,7},{7,0},{8,9},{9,10},{10,1... | collective-permute-start | bytes 38024 | tf_op jit(solution)/shard_map/ppermute | solution.py:14
  37.1 3.5 %collective-permute-start.7 = (f32[6,1,528]{2,0,1:T(8,128)S(1)}, f32[6,1,528]{2,0,1:T(8,128)S(1)}, u32[]{:S(2)}, u32[]{:S(2)}) collective-permute-start(f32[6,1,528]{2,0,1:T(8,128)S(1)} %get-tuple-element.369), channel_id=1, source_target_pairs={{1,0},{2,1},{3,2},{4,3},{5,4},{6,5},{7,6},{0,7},{9,8},{10,9},{11,1... | collective-permute-start | bytes 38024 | tf_op jit(solution)/shard_map/ppermute | solution.py:17
  40.8 1.5 %collective-permute-done.6 = f32[6,1,528]{2,0,1:T(8,128)S(1)} collective-permute-done((f32[6,1,528]{2,0,1:T(8,128)S(1)}, f32[6,1,528]{2,0,1:T(8,128)S(1)}, u32[]{:S(2)}, u32[]{:S(2)}) %collective-permute-start.6) | collective-permute-done | bytes 12704 | tf_op jit(solution)/shard_map/ppermute | solution.py:14
  43.0 1.2 %fusion.17 = f32[4,32,528]{2,0,1:T(4,128)S(1)} fusion(f32[6,33,528]{2,0,1:T(8,128)S(1)} %get-tuple-element.367, f32[6,33,528]{2,0,1:T(8,128)S(1)} %get-tuple-element.366, f32[1,32,528]{2,0,1:T(1,128)S(1)} %collective-permute-done.5, f32[4,32,528]{2,0,1:T(4,128)S(1)} %fusion.11, f32[1,32,528]{2,0,1:T(1,128)S(1)} %collective-permute-done.4, ...), kind=kLoop, calls=%fused_computation.48 | loop fusion | flops 1419264 | bytes 2571400 | tf_op jit(solution)/shard_map/sub | solution.py:153
  44.2 1.5 %gather_fusion.1 = f32[128,528]{1,0:T(8,128)} fusion(f32[128,528]{1,0:T(8,128)S(1)} %bitcast.130, s32[1024]{0:T(1024)S(1)} %pad_clamp_fusion.2), kind=kCustom, calls=%fused_computation.4 | custom fusion | bytes 541184 | tf_op jit(solution)/shard_map/gather | solution.py:168
  45.7 3.5 %all-to-all-start.1 = ((f32[4,32,528]{2,1,0:T(8,128)}), f32[4,32,528]{2,1,0:T(8,128)S(1)}, u32[]{:S(2)}, u32[]{:S(2)}) async-start(f32[4,32,528]{2,1,0:T(8,128)} %bitcast.16), calls=%async_computation.1 | async-start | bytes 655360 | tf_op jit(solution)/shard_map/all_to_all | solution.py:170
  49.4 1.3 %gather_fusion.4 = f32[128,48]{1,0:T(8,128)} fusion(f32[48,128]{0,1:T(8,128)S(1)} %bitcast.136, s32[1024]{0:T(1024)S(1)} %pad_clamp_fusion.1), kind=kCustom, calls=%fused_computation.1.clone | custom fusion | bytes 49664 | tf_op jit(solution)/shard_map/jit(_take)/gather | solution.py:179
  51.3 4.6 %all-to-all-done.1 = f32[4,32,528]{2,1,0:T(8,128)S(1)} async-done(((f32[4,32,528]{2,1,0:T(8,128)}), f32[4,32,528]{2,1,0:T(8,128)S(1)}, u32[]{:S(2)}, u32[]{:S(2)}) %all-to-all-start.1) | async-done | bytes 270368 | tf_op jit(solution)/shard_map/all_to_all | solution.py:170
  57.0 5.6 %while.47 = (s32[]{:T(128)}, f32[128]{0:T(128)S(1)}, f32[11,128]{1,0:T(8,128)S(1)}, f32[48,128]{1,0:T(8,128)S(1)}, f32[48,11,128]{2,1,0:T(8,128)S(1)}, /*index=5...) while((s32[]{:T(128)}, f32[128]{0:T(128)S(1)}, ...), condition=%wide.region_2.4_spmd.clone, body=%wide.region_1.3_spmd.clone.sunk | while | flops 6147 | bytes 39048 | solution.py:107
  62.7 2.7 %while.48 = (s32[]{:T(128)}, f32[11,128]{1,0:T(8,128)S(1)}, f32[48,11,128]{2,1,0:T(8,128)S(1)}, f32[48,11,128]{2,1,0:T(8,128)S(1)}, f32[48,128]{1,0:T(8,128)S(1)}, /*index=5*/s32[]{:T(128)}, s32[]{:T(128)}, s32[]{:T(128)}) while((s32[]{:T(128)}, f32[11,128]{1,0:T(8,128)S(1)}, f32[48,11,128]{2,1,0:T(8,128)S(1)}, ...), condition=%wide.region_4.6_spmd.clone, body=%wide.region_3.5_spmd.clone.sunk | while | flops 4228 | bytes 34419 | solution.py:114
  66.2 0.9 multiply_add_fusion
  67.2 35.4 %while.49 = (s32[]{:T(128)}, f32[128]{0:T(128)S(1)}, f32[48,128]{1,0:T(8,128)S(1)}, f32[48,128]{1,0:T(8,128)}, f32[48,128]{1,0:T(8,128)S(1)}, /*index=5*/s32[]{:T(128)}, s32[]{:T(128)}) while((s32[]{:T(128)}, f32[128]{0:T(128)S(1)}, f32[48,128]{1,0:T(8,128)S(1)}, f32[48,128]{1,0:T(8,128)}, f32[48,128]{1,0:T(8,128)S(1)}, ...), condition=%wide.region_6.8_spmd.clone, body=%wide.region_5.7_spmd.clone.sunk | while | flops 643 | bytes 3679 | solution.py:134
  103.2 1.0 reshape.178
  104.3 3.5 %all-to-all-start.2 = ((f32[4,32,528]{2,1,0:T(8,128)}), f32[4,32,528]{2,1,0:T(8,128)S(1)}, u32[]{:S(2)}, u32[]{:S(2)}) async-start(f32[4,32,528]{2,1,0:T(8,128)} %reshape.178), calls=%async_computation.2 | async-start | bytes 655360 | tf_op jit(solution)/shard_map/all_to_all | solution.py:182
  107.8 6.7 %all-to-all-done.2 = f32[4,32,528]{2,1,0:T(8,128)S(1)} async-done(((f32[4,32,528]{2,1,0:T(8,128)}), f32[4,32,528]{2,1,0:T(8,128)S(1)}, u32[]{:S(2)}, u32[]{:S(2)}) %all-to-all-start.2) | async-done | bytes 270368 | tf_op jit(solution)/shard_map/all_to_all | solution.py:182
  114.5 0.8 gather_fusion.2
  115.5 0.7 copy.120
  (469 shorter events, 54.0 us)
Async XLA Ops:
  0.8 1.1 copy-start.4
  2.5 1.0 copy-start
  2.5 1.0 copy-start.5
  4.5 2.5 %copy-start.8 = (s32[4,32]{1,0:T(4,128)S(1)}, s32[4,32]{1,0:T(4,128)}, u32[]{:S(2)}) copy-start(s32[4,32]{1,0:T(4,128)} %param.22) | copy-start | bytes 1540
  4.5 16.9 %collective-permute-start = (f32[1,32,528]{2,0,1:T(1,128)S(1)}, f32[1,32,528]{2,0,1:T(1,128)S(1)}, u32[]{:S(2)}, u32[]{:S(2)}) collective-permute-start(f32[1,32,528]{2,0,1:T(1,128)S(1)} %get-tuple-element.376), channel_id=1, source_target_pairs={{0,8},{8,16},{16,24},{24,0},{1,9},{9,17},{17,25},{25,1},{2,10},{10... | collective-permute-start | bytes 202760 | tf_op jit(solution)/shard_map/ppermute | solution.py:14
  5.0 16.4 %collective-permute-start.1 = (f32[1,32,528]{2,0,1:T(1,128)S(1)}, f32[1,32,528]{2,0,1:T(1,128)S(1)}, u32[]{:S(2)}, u32[]{:S(2)}) collective-permute-start(f32[1,32,528]{2,0,1:T(1,128)S(1)} %get-tuple-element.377), channel_id=1, source_target_pairs={{8,0},{16,8},{24,16},{0,24},{9,1},{17,9},{25,17},{1,25},{10,2},{18... | collective-permute-start | bytes 202760 | tf_op jit(solution)/shard_map/ppermute | solution.py:17
  11.5 8.6 %all-to-all-start = ((s32[4,1,32]{2,1,0:T(1,128)}), s32[4,1,32]{2,1,0:T(1,128)S(1)}, u32[]{:S(2)}, u32[]{:S(2)}) async-start(s32[4,1,32]{2,1,0:T(1,128)} %bitcast.12), calls=%async_computation | async-start | bytes 4096 | tf_op jit(solution)/shard_map/all_to_all | solution.py:171
  15.1 0.9 copy-start.1
  15.2 0.7 copy-start.7
  16.0 0.7 copy-start.2
  16.7 0.7 copy-start.3
  21.5 6.9 %collective-permute-start.2 = (f32[6,1,528]{2,0,1:T(8,128)S(1)}, f32[6,1,528]{2,0,1:T(8,128)S(1)}, u32[]{:S(2)}, u32[]{:S(2)}) collective-permute-start(f32[6,1,528]{2,0,1:T(8,128)S(1)} %get-tuple-element.372), channel_id=1, source_target_pairs={{0,1},{1,2},{2,3},{3,4},{4,5},{5,6},{6,7},{7,0},{8,9},{9,10},{10,1... | collective-permute-start | bytes 38024 | tf_op jit(solution)/shard_map/ppermute | solution.py:14
  23.5 4.8 %collective-permute-start.3 = (f32[6,1,528]{2,0,1:T(8,128)S(1)}, f32[6,1,528]{2,0,1:T(8,128)S(1)}, u32[]{:S(2)}, u32[]{:S(2)}) collective-permute-start(f32[6,1,528]{2,0,1:T(8,128)S(1)} %get-tuple-element.373), channel_id=1, source_target_pairs={{1,0},{2,1},{3,2},{4,3},{5,4},{6,5},{7,6},{0,7},{9,8},{10,9},{11,1... | collective-permute-start | bytes 38024 | tf_op jit(solution)/shard_map/ppermute | solution.py:17
  31.4 3.9 %collective-permute-start.4 = (f32[1,32,528]{2,0,1:T(1,128)S(1)}, f32[1,32,528]{2,0,1:T(1,128)S(1)}, u32[]{:S(2)}, u32[]{:S(2)}) collective-permute-start(f32[1,32,528]{2,0,1:T(1,128)S(1)} %get-tuple-element.374), channel_id=1, source_target_pairs={{0,8},{8,16},{16,24},{24,0},{1,9},{9,17},{17,25},{25,1},{2,10},{10... | collective-permute-start | bytes 202760 | tf_op jit(solution)/shard_map/ppermute | solution.py:14
  31.4 4.2 %collective-permute-start.5 = (f32[1,32,528]{2,0,1:T(1,128)S(1)}, f32[1,32,528]{2,0,1:T(1,128)S(1)}, u32[]{:S(2)}, u32[]{:S(2)}) collective-permute-start(f32[1,32,528]{2,0,1:T(1,128)S(1)} %get-tuple-element.375), channel_id=1, source_target_pairs={{8,0},{16,8},{24,16},{0,24},{9,1},{17,9},{25,17},{1,25},{10,2},{18... | collective-permute-start | bytes 202760 | tf_op jit(solution)/shard_map/ppermute | solution.py:17
  35.7 6.6 %collective-permute-start.6 = (f32[6,1,528]{2,0,1:T(8,128)S(1)}, f32[6,1,528]{2,0,1:T(8,128)S(1)}, u32[]{:S(2)}, u32[]{:S(2)}) collective-permute-start(f32[6,1,528]{2,0,1:T(8,128)S(1)} %get-tuple-element.368), channel_id=1, source_target_pairs={{0,1},{1,2},{2,3},{3,4},{4,5},{5,6},{6,7},{7,0},{8,9},{9,10},{10,1... | collective-permute-start | bytes 38024 | tf_op jit(solution)/shard_map/ppermute | solution.py:14
  37.1 5.2 %collective-permute-start.7 = (f32[6,1,528]{2,0,1:T(8,128)S(1)}, f32[6,1,528]{2,0,1:T(8,128)S(1)}, u32[]{:S(2)}, u32[]{:S(2)}) collective-permute-start(f32[6,1,528]{2,0,1:T(8,128)S(1)} %get-tuple-element.369), channel_id=1, source_target_pairs={{1,0},{2,1},{3,2},{4,3},{5,4},{6,5},{7,6},{0,7},{9,8},{10,9},{11,1... | collective-permute-start | bytes 38024 | tf_op jit(solution)/shard_map/ppermute | solution.py:17
  42.3 0.7 copy-start.6
  45.7 10.2 %all-to-all-start.1 = ((f32[4,32,528]{2,1,0:T(8,128)}), f32[4,32,528]{2,1,0:T(8,128)S(1)}, u32[]{:S(2)}, u32[]{:S(2)}) async-start(f32[4,32,528]{2,1,0:T(8,128)} %bitcast.16), calls=%async_computation.1 | async-start | bytes 655360 | tf_op jit(solution)/shard_map/all_to_all | solution.py:170
  104.3 10.2 %all-to-all-start.2 = ((f32[4,32,528]{2,1,0:T(8,128)}), f32[4,32,528]{2,1,0:T(8,128)S(1)}, u32[]{:S(2)}, u32[]{:S(2)}) async-start(f32[4,32,528]{2,1,0:T(8,128)} %reshape.178), calls=%async_computation.2 | async-start | bytes 655360 | tf_op jit(solution)/shard_map/all_to_all | solution.py:182
where the time goes:
time: 118 us; the launch traced here: 116 us
  other arithmetic  46 us (39%)
  starting transfers between devices  24.8 us (21%)
  local copies, waits for them, and re-layouts  22.4 us (19%)
  waiting for transfers between devices  15.7 us (13%)
  loops' own time  4.04 us (3%)
  matrix products  2.9 us (2%)
    mul x48, other arithmetic, settle(): return (fall_k * settled, settled)  33.3 us
    ppermute x4, starting transfers between devices, extended(): lax.ppermute(lax.slice_in_dim(block, 0, width, axis=dim), axis, backward)  10.3 us
    all_to_all x1, waiting for transfers between devices, local(): lax.all_to_all(tendency, 'gx', split_axis=0, concat_axis=0, tiled=True)  6.68 us
    unnamed x28, local copies, waits for them, and re-layouts  5.66 us
    all_to_all x1, waiting for transfers between devices, local(): lax.all_to_all(packed, 'gx', split_axis=0, concat_axis=0, tiled=True)  4.64 us
    ppermute x4, starting transfers between devices, extended(): lax.ppermute(lax.slice_in_dim(block, block.shape[dim] - width, None, axis...  4.06 us
    ppermute x4, waiting for transfers between devices, extended(): lax.ppermute(lax.slice_in_dim(block, block.shape[dim] - width, None, axis...  3.96 us
    all_to_all x1, starting transfers between devices, local(): lax.all_to_all(sent_slots, 'gx', split_axis=0, concat_axis=0, tiled=True)  3.51 us
  transfers between devices with their start and end apart: 11, of which 6 were waited for; matrix products, arithmetic and copies ran while one was open for 10% of the time, Pallas kernels for 0%

commit v1 on v0

v1 whole, which is shorter than its diff:
```python
import functools

import jax
import jax.numpy as jnp
import numpy as np
from jax import lax
from jax.experimental import pallas as pl
from jax.experimental.pallas import tpu as pltpu
from jax.sharding import PartitionSpec as P

VMEM = pl.BlockSpec(memory_space=pltpu.VMEM)
PARAMS = pltpu.CompilerParams(vmem_limit_bytes=16 * 1024 * 1024)


def second_table():
    nodes = np.array([-1.0, -1.0 / np.sqrt(5.0), 1.0 / np.sqrt(5.0), 1.0])
    deriv = np.zeros((4, 4))
    for i in range(4):
        for j in range(4):
            if i == j:
                deriv[i, j] = sum(1.0 / (nodes[i] - nodes[k]) for k in range(4) if k != i)
            else:
                upper = np.prod([nodes[i] - nodes[k] for k in range(4) if k != i])
                lower = np.prod([nodes[j] - nodes[k] for k in range(4) if k != j])
                deriv[i, j] = upper / (lower * (nodes[i] - nodes[j]))
    return deriv @ deriv


def laplacian_tables(size_x, size_y):
    second = second_table()
    lap = np.kron(np.kron(np.eye(size_x // 4), second), np.eye(size_y))
    lap = lap + np.kron(np.eye(size_x), np.kron(np.eye(size_y // 4), second))
    partner = np.zeros_like(lap)
    for x in range(size_x):
        for y in range(size_y):
            other = y - 1 if y % 4 == 0 else y + 1 if y % 4 == 3 else -1
            if 0 <= other < size_y:
                partner[x * size_y + y] = lap[x * size_y + other]
    return np.stack([lap, partner]).astype(np.float32)


def split(value):
    high = value.astype(jnp.bfloat16)
    return high, (value - high.astype(jnp.float32)).astype(jnp.bfloat16)


def product(left, right):
    left_high, left_low = left
    right_high, right_low = right
    dot = functools.partial(jnp.dot, preferred_element_type=jnp.float32)
    return dot(left_high, right_high) + (dot(left_high, right_low) + dot(left_low, right_high))


def to_column(plane, partner=False):
    size_x, size_y = plane.shape
    row = lax.broadcasted_iota(jnp.int32, (size_y, size_y), 0)
    lane = lax.broadcasted_iota(jnp.int32, (size_y, size_y), 1)
    if partner:
        row = jnp.where(row % 4 == 0, row - 1, jnp.where(row % 4 == 3, row + 1, -1))
    pick = row == lane
    parts = [
        jnp.sum(jnp.where(pick, plane[x : x + 1, :], 0.0), axis=1, keepdims=True)
        for x in range(size_x)
    ]
    return jnp.concatenate(parts, axis=0)


def operator(tables, mass):
    return split(to_column(mass) * tables[0] + to_column(mass, True) * tables[1])


def emit(total, size_x, size_y, refs):
    x_low, x_high, y_low, y_high, c_ll, c_lh, c_hl, c_hh = refs
    last = (size_x - 1) * size_y
    x_low[...] = total[:size_y]
    x_high[...] = total[last:]
    for x in range(size_x):
        y_low[x : x + 1, :] = total[x * size_y : x * size_y + 1]
        y_high[x : x + 1, :] = total[(x + 1) * size_y - 1 : (x + 1) * size_y]
    c_ll[...] = total[:1]
    c_lh[...] = total[size_y - 1 : size_y]
    c_hl[...] = total[last : last + 1]
    c_hh[...] = total[last + size_y - 1 :]


def absorb(total_ref, size_x, size_y, refs):
    x_low, x_high, y_low, y_high, c_ll, c_lh, c_hl, c_hh = refs
    last = (size_x - 1) * size_y
    total_ref[:size_y] += x_low[...]
    total_ref[last:] += x_high[...]
    for x in range(size_x):
        first, final = x * size_y, (x + 1) * size_y - 1
        total_ref[first : first + 1, :] += y_low[x : x + 1, :]
        total_ref[final : final + 1, :] += y_high[x : x + 1, :]
    total_ref[:1] += c_ll[...]
    total_ref[size_y - 1 : size_y] += c_lh[...]
    total_ref[last : last + 1] += c_hl[...]
    total_ref[last + size_y - 1 :] += c_hh[...]


def first_kernel(size_x, size_y, state, mass, tables, total, *messages):
    result = product(operator(tables, mass[...]), split(state[...]))
    total[...] = result
    emit(result, size_x, size_y, messages)


def second_kernel(size_x, size_y, total, mass, inverse, tables, *refs):
    halos, result_ref, messages, work = refs[:8], refs[8], refs[9:17], refs[17]
    work[...] = total[...]
    absorb(work, size_x, size_y, halos)
    once = to_column(inverse[...]) * work[...]
    result = product(operator(tables, mass[...]), split(once))
    result_ref[...] = result
    emit(result, size_x, size_y, messages)


def third_kernel(size_x, size_y, levels, state, hyper, total, inverse, factors, *refs):
    halos, out, work, turned, values = refs[:8], refs[8], refs[9], refs[10], refs[11]
    columns, width = state.shape
    variables = width // levels
    work[...] = total[...]
    absorb(work, size_x, size_y, halos)
    dynamic = state[...] - hyper[...] * (to_column(inverse[...]) * work[...])
    turned[...] = dynamic.T
    scale, down, up, keep, flow, cloud = (
        factors.at[i * levels : (i + 1) * levels] for i in range(6)
    )
    value = jnp.zeros((variables, columns), jnp.float32)
    for k in range(levels):
        rows = turned[pl.ds(k, variables, stride=levels), :]
        value = rows * scale[k : k + 1, :] + down[k : k + 1, :] * value
        values[k, :variables, :] = value
    solved = jnp.zeros((variables, columns), jnp.float32)
    for k in reversed(range(levels)):
        solved = values[k, :variables, :] + up[k : k + 1, :] * solved
        turned[pl.ds(k, variables, stride=levels), :] = solved
    heat, vapour, liquid = (turned.at[i * levels : (i + 1) * levels] for i in range(3))
    condensed = cloud[...] * 0.5 * jnp.maximum(vapour[...] - 0.3 * heat[...], 0.0)
    vapour[...] = vapour[...] - condensed
    heat[...] = heat[...] + 2.0 * condensed
    liquid[...] = (liquid[...] + condensed) * keep[...]
    settled = jnp.zeros((1, columns), jnp.float32)
    for k in range(levels):
        settled = liquid[k : k + 1, :] + flow[k : k + 1, :] * settled
        liquid[k : k + 1, :] = settled
    out[...] = turned[...].T


def factor_kernel(levels, slots, diff, fall, cloud, factors):
    peers, _, span = diff.shape
    size_x, size_y = slots.shape
    columns = size_x * size_y
    picked = [jnp.zeros((levels, columns), jnp.float32) for _ in range(3)]
    wanted = jnp.concatenate([slots[x : x + 1, :] for x in range(size_x)], axis=1)
    for peer in range(peers):
        entry = lax.broadcasted_iota(jnp.int32, (span, columns), 0) + peer * span
        choice = (entry == wanted).astype(jnp.float32).astype(jnp.bfloat16)
        for i, source in enumerate((diff, fall, cloud)):
            rest = source[peer]
            for _ in range(3):
                part = rest.astype(jnp.bfloat16)
                rest = rest - part.astype(jnp.float32)
                picked[i] = picked[i] + jnp.dot(part, choice, preferred_element_type=jnp.float32)
    mixing, falling, covered = picked
    scale, down, up, keep, flow, cover = (
        factors.at[i * levels : (i + 1) * levels] for i in range(6)
    )
    gain = jnp.zeros((1, columns), jnp.float32)
    for k in range(levels):
        above = mixing[k : k + 1] if k else jnp.zeros_like(gain)
        below = mixing[k + 1 : k + 2] if k + 1 < levels else jnp.zeros_like(gain)
        centre = 1.0 + above + (below if k + 1 < levels else mixing[:1])
        inverse = 1.0 / (centre - above * gain)
        gain = below * inverse
        scale[k : k + 1, :] = inverse
        down[k : k + 1, :] = above * inverse
        up[k : k + 1, :] = gain
    kept = 1.0 / (1.0 + falling)
    keep[...] = kept
    flow[:1, :] = jnp.zeros((1, columns), jnp.float32)
    flow[1:, :] = falling[:-1] * kept[1:]
    cover[...] = covered


def neighbours(messages):
    size_gx, size_gy = lax.axis_size("gx"), lax.axis_size("gy")
    x_low, x_high, y_low, y_high, c_ll, c_lh, c_hl, c_hh = messages

    def send(value, step_x, step_y):
        pairs = [
            (
                i * size_gy + j,
                (i + step_x) % size_gx * size_gy + (j + step_y) % size_gy,
            )
            for i in range(size_gx)
            for j in range(size_gy)
        ]
        return lax.ppermute(value, ("gx", "gy"), pairs)

    return (
        send(x_high, 1, 0),
        send(x_low, -1, 0),
        send(y_high, 0, 1),
        send(y_low, 0, -1),
        send(c_hh, 1, 1),
        send(c_hl, 1, -1),
        send(c_lh, -1, 1),
        send(c_ll, -1, -1),
    )


def local(
    model_state, hyper_coef, point_mass, inverse_mass, span_slot, vert_diff, fall_rate, cloud_frac
):
    size_x, size_y, width = model_state.shape
    levels = vert_diff.shape[1]
    columns = size_x * size_y
    state = model_state.reshape(columns, width)
    hyper = hyper_coef.reshape(1, width)
    tables = jnp.asarray(laplacian_tables(size_x, size_y))

    def array(*shape):
        return jax.ShapeDtypeStruct(shape, jnp.float32)

    whole = array(columns, width)
    messages = [array(size_y, width)] * 2 + [array(size_x, width)] * 2 + [array(1, width)] * 4

    diff, fall, cloud = (
        lax.all_gather(value[0], "gx") for value in (vert_diff, fall_rate, cloud_frac)
    )
    factors = pl.pallas_call(
        functools.partial(factor_kernel, levels),
        out_shape=array(6 * levels, columns),
        in_specs=[VMEM] * 4,
        out_specs=VMEM,
        compiler_params=PARAMS,
        name="factors",
    )(span_slot, diff, fall, cloud)

    total, *sent = pl.pallas_call(
        functools.partial(first_kernel, size_x, size_y),
        out_shape=[whole] + messages,
        in_specs=[VMEM] * 3,
        out_specs=[VMEM] * 9,
        compiler_params=PARAMS,
        name="first",
    )(state, point_mass, tables)
    arrived = neighbours(sent)
    total, *sent = pl.pallas_call(
        functools.partial(second_kernel, size_x, size_y),
        out_shape=[whole] + messages,
        in_specs=[VMEM] * 12,
        out_specs=[VMEM] * 9,
        scratch_shapes=[pltpu.VMEM((columns, width), jnp.float32)],
        compiler_params=PARAMS,
        name="second",
    )(total, point_mass, inverse_mass, tables, *arrived)
    arrived = neighbours(sent)
    result = pl.pallas_call(
        functools.partial(third_kernel, size_x, size_y, levels),
        out_shape=whole,
        in_specs=[VMEM] * 13,
        out_specs=VMEM,
        scratch_shapes=[
            pltpu.VMEM((columns, width), jnp.float32),
            pltpu.VMEM((width, columns), jnp.float32),
            pltpu.VMEM((levels, 16, columns), jnp.float32),
        ],
        compiler_params=PARAMS,
        name="third",
    )(state, hyper, total, inverse_mass, factors, *arrived)
    return result.reshape(size_x, size_y, width)


def solution(mesh):
    placed = (
        P("gx", "gy", None),
        P(),
        P("gx", "gy"),
        P("gx", "gy"),
        P("gx", "gy"),
        P("gy", None, "gx"),
        P("gy", None, "gx"),
        P("gy", None, "gx"),
    )
    return jax.shard_map(
        local, mesh=mesh, in_specs=placed, out_specs=P("gx", "gy", None), check_vma=False
    )
```

time: 118 us -> 50 us (0.42); the launches traced: 116 us -> 49.8 us
  other arithmetic: 46 us -> 0 us
  local copies, waits for them, and re-layouts: 22.4 us -> 2.6 us
  blocking collectives: 0 us -> 16.5 us
  waiting for transfers between devices: 15.7 us -> 1.15 us
  loops' own time: 4.04 us -> 0 us
  Pallas kernels: 0 us -> 3.38 us
  matrix products: 2.9 us -> 0 us
    mul x49 -> x0, other arithmetic: 34.3 us -> none  [the longest x48 33.3 us: settle(): return (fall_k * settled, settled)]
    all_gather x0 -> x3, blocking collectives: none -> 16.5 us  [local(): lax.all_gather(value[0], 'gx')]
    ppermute x8 -> x16, starting transfers between devices: 14.3 us -> 25.9 us  [send(): return lax.ppermute(value, ('gx', 'gy'), pairs)]
    all_to_all x3 -> x0, waiting for transfers between devices: 11.3 us -> none  [the longest x1 6.68 us: local(): lax.all_to_all(tendency, 'gx', split_axis=0, concat_axis=0, tiled=True)]
    all_to_all x3 -> x0, starting transfers between devices: 10.5 us -> none  [the longest x1 3.51 us: local(): lax.all_to_all(sent_slots, 'gx', split_axis=0, concat_axis=0, tiled=True)]
    gather x6 -> x0, local copies, waits for them, and re-layouts: 6.11 us -> none  [the longest x1 1.53 us: local(): packed = flat_state[owner_order].reshape(peers, per_peer, row_width)]
    sort x2 -> x0, other arithmetic: 5.15 us -> none  [the longest x1 2.62 us: local(): inverse_order = jnp.argsort(owner_order)]
    another operation x3 -> x0, loops' own time: 4.04 us -> none  [the longest x1 1.64 us: physics(): lax.scan(backward, jnp.zeros_like(fields[0]), (gains, values), reverse=True)]
  transfers between devices with their start and end apart: 11 -> 16, of which waited for: 6 -> 2; matrix products, arithmetic and copies ran while one was open for 10% -> 0% of each run, Pallas kernels for 0% -> 2%
where the time goes in v1:
time: 50 us; the launch traced here: 49.8 us
  starting transfers between devices  25.9 us (52%)
  blocking collectives  16.5 us (33%)
  Pallas kernels  3.38 us (7%)
  local copies, waits for them, and re-layouts  2.6 us (5%)
  waiting for transfers between devices  1.15 us (2%)
    ppermute x16, starting transfers between devices, send(): return lax.ppermute(value, ('gx', 'gy'), pairs)  25.9 us
    all_gather x3, blocking collectives, local(): lax.all_gather(value[0], 'gx')  16.5 us
    unnamed x22, local copies, waits for them, and re-layouts  2.6 us
    pallas_call x1, Pallas kernels, local(): pl.pallas_call(functools.partial(third_kernel, size_x, size_y, levels), o...  1.53 us
    ppermute x16, waiting for transfers between devices, send(): return lax.ppermute(value, ('gx', 'gy'), pairs)  1.15 us
  transfers between devices with their start and end apart: 16, of which 2 were waited for; matrix products, arithmetic and copies ran while one was open for 0% of the time, Pallas kernels for 2%

profile of v1, /device:TPU:0, one launch (start us, length us, event | category | flops | bytes accessed | tf_op | source)
XLA Modules:
  0.0 49.8 jit_solution(9127428714765973704)
XLA Ops:
  0.0 1.0 %copy-done = f32[4,32,528]{2,1,0:T(8,128)S(1)} copy-done((f32[4,32,528]{2,1,0:T(8,128)S(1)}, f32[4,32,528]{2,1,0:T(8,128)}, u32[]{:S(2)}) %copy-start) | copy-done | bytes 270360
  1.0 0.9 %copy-done.2 = f32[2,128,128]{2,1,0:T(8,128)S(1)} copy-done((f32[2,128,128]{2,1,0:T(8,128)S(1)}, f32[2,128,128]{2,1,0:T(8,128)}, u32[]{:S(2)}) %copy-start.2) | copy-done | bytes 131096
  1.9 0.7 %copy-done.4 = f32[4,32]{1,0:T(4,128)S(1)} copy-done((f32[4,32]{1,0:T(4,128)S(1)}, f32[4,32]{1,0:T(4,128)}, u32[]{:S(2)}) %copy-start.4) | copy-done | bytes 536
  2.6 0.4 first.1
  3.0 0.0 copy-start.3
  3.0 0.5 %collective-permute-start = (f32[32,528]{1,0:T(8,128)S(1)}, f32[32,528]{1,0:T(8,128)S(1)}, u32[]{:S(2)}, u32[]{:S(2)}) collective-permute-start(f32[32,528]{1,0:T(8,128)S(1)} %get-tuple-element.24), channel_id=1, source_target_pairs={{0,8},{1,9},{2,10},{3,11},{4,12},{5,13},{6,14},{7,15},{8,16},{9,17... | collective-permute-start | bytes 202760 | tf_op jit(solution)/shard_map/ppermute | solution.py:198
  3.5 2.0 %collective-permute-start.1 = (f32[32,528]{1,0:T(8,128)S(1)}, f32[32,528]{1,0:T(8,128)S(1)}, u32[]{:S(2)}, u32[]{:S(2)}) collective-permute-start(f32[32,528]{1,0:T(8,128)S(1)} %get-tuple-element.25), channel_id=1, source_target_pairs={{0,24},{1,25},{2,26},{3,27},{4,28},{5,29},{6,30},{7,31},{8,0},{9,1... | collective-permute-start | bytes 202760 | tf_op jit(solution)/shard_map/ppermute | solution.py:198
  5.5 1.7 %collective-permute-start.4 = (f32[1,528]{1,0:T(1,128)S(1)}, f32[1,528]{1,0:T(1,128)S(1)}, u32[]{:S(2)}, u32[]{:S(2)}) collective-permute-start(f32[1,528]{1,0:T(1,128)S(1)} %get-tuple-element.28), channel_id=1, source_target_pairs={{0,9},{1,10},{2,11},{3,12},{4,13},{5,14},{6,15},{7,8},{8,17},{9,18... | collective-permute-start | bytes 6344 | tf_op jit(solution)/shard_map/ppermute | solution.py:198
  7.3 4.4 %collective-permute-start.5 = (f32[1,528]{1,0:T(1,128)S(1)}, f32[1,528]{1,0:T(1,128)S(1)}, u32[]{:S(2)}, u32[]{:S(2)}) collective-permute-start(f32[1,528]{1,0:T(1,128)S(1)} %get-tuple-element.29), channel_id=1, source_target_pairs={{0,15},{1,8},{2,9},{3,10},{4,11},{5,12},{6,13},{7,14},{8,23},{9,16... | collective-permute-start | bytes 6344 | tf_op jit(solution)/shard_map/ppermute | solution.py:198
  11.6 0.0 collective-permute-start.6
  11.7 0.5 collective-permute-done.4.refs_4_
  12.1 0.2 collective-permute-start.2
  12.3 0.6 %collective-permute-done.5.refs_5_ = f32[1,528]{1,0:T(1,128)S(1)} collective-permute-done((f32[1,528]{1,0:T(1,128)S(1)}, f32[1,528]{1,0:T(1,128)S(1)}, u32[]{:S(2)}, u32[]{:S(2)}) %collective-permute-start.5) | collective-permute-done | bytes 2144 | tf_op jit(solution)/shard_map/ppermute | solution.py:198
  13.0 4.5 %collective-permute-start.3 = (f32[4,528]{1,0:T(4,128)S(1)}, f32[4,528]{1,0:T(4,128)S(1)}, u32[]{:S(2)}, u32[]{:S(2)}) collective-permute-start(f32[4,528]{1,0:T(4,128)S(1)} %get-tuple-element.27), channel_id=1, source_target_pairs={{0,7},{1,0},{2,1},{3,2},{4,3},{5,4},{6,5},{7,6},{8,15},{9,8},{10,9... | collective-permute-start | bytes 25352 | tf_op jit(solution)/shard_map/ppermute | solution.py:198
  17.5 0.0 collective-permute-done.6.refs_6_
  17.5 0.0 copy-start.5
  17.5 5.8 %all_gather.10.fall = f32[4,48,128]{2,1,0:T(8,128)S(1)} all-gather(f32[1,48,128]{2,1,0:T(8,128)S(1)} %copy-done.7), channel_id=1, replica_groups=mesh['gx'=4,'gy'=8] {'gx'}, dimensions={0}, use_global_device_ids=true | all-gather | bytes 122880 | tf_op jit(solution)/shard_map/all_gather | solution.py:229
  23.3 0.0 copy-start.8
  23.3 0.0 copy-start.10
  23.3 0.0 copy-start.6
  23.3 0.5 second.1
  23.8 0.4 collective-permute-start.8
  24.2 1.4 %collective-permute-start.9 = (f32[32,528]{1,0:T(8,128)S(1)}, f32[32,528]{1,0:T(8,128)S(1)}, u32[]{:S(2)}, u32[]{:S(2)}) collective-permute-start(f32[32,528]{1,0:T(8,128)S(1)} %get-tuple-element.34), channel_id=1, source_target_pairs={{0,24},{1,25},{2,26},{3,27},{4,28},{5,29},{6,30},{7,31},{8,0},{9,1... | collective-permute-start | bytes 202760 | tf_op jit(solution)/shard_map/ppermute | solution.py:198
  25.6 1.8 %collective-permute-start.12 = (f32[1,528]{1,0:T(1,128)S(1)}, f32[1,528]{1,0:T(1,128)S(1)}, u32[]{:S(2)}, u32[]{:S(2)}) collective-permute-start(f32[1,528]{1,0:T(1,128)S(1)} %get-tuple-element.37), channel_id=1, source_target_pairs={{0,9},{1,10},{2,11},{3,12},{4,13},{5,14},{6,15},{7,8},{8,17},{9,18... | collective-permute-start | bytes 6344 | tf_op jit(solution)/shard_map/ppermute | solution.py:198
  27.4 3.4 %collective-permute-start.13 = (f32[1,528]{1,0:T(1,128)S(1)}, f32[1,528]{1,0:T(1,128)S(1)}, u32[]{:S(2)}, u32[]{:S(2)}) collective-permute-start(f32[1,528]{1,0:T(1,128)S(1)} %get-tuple-element.38), channel_id=1, source_target_pairs={{0,15},{1,8},{2,9},{3,10},{4,11},{5,12},{6,13},{7,14},{8,23},{9,16... | collective-permute-start | bytes 6344 | tf_op jit(solution)/shard_map/ppermute | solution.py:198
  30.9 5.5 %all_gather.11.cloud = f32[4,48,128]{2,1,0:T(8,128)S(1)} all-gather(f32[1,48,128]{2,1,0:T(8,128)S(1)} %copy-done.8), channel_id=1, replica_groups=mesh['gx'=4,'gy'=8] {'gx'}, dimensions={0}, use_global_device_ids=true | all-gather | bytes 122880 | tf_op jit(solution)/shard_map/all_gather | solution.py:229
  36.3 0.5 collective-permute-start.10
  36.8 4.2 %collective-permute-start.11 = (f32[4,528]{1,0:T(4,128)S(1)}, f32[4,528]{1,0:T(4,128)S(1)}, u32[]{:S(2)}, u32[]{:S(2)}) collective-permute-start(f32[4,528]{1,0:T(4,128)S(1)} %get-tuple-element.36), channel_id=1, source_target_pairs={{0,7},{1,0},{2,1},{3,2},{4,3},{5,4},{6,5},{7,6},{8,15},{9,8},{10,9... | collective-permute-start | bytes 25352 | tf_op jit(solution)/shard_map/ppermute | solution.py:198
  41.1 0.9 %collective-permute-start.15 = (f32[1,528]{1,0:T(1,128)S(1)}, f32[1,528]{1,0:T(1,128)S(1)}, u32[]{:S(2)}, u32[]{:S(2)}) collective-permute-start(f32[1,528]{1,0:T(1,128)S(1)} %get-tuple-element.40), channel_id=1, source_target_pairs={{0,31},{1,24},{2,25},{3,26},{4,27},{5,28},{6,29},{7,30},{8,7},{9,0... | collective-permute-start | bytes 6344 | tf_op jit(solution)/shard_map/ppermute | solution.py:198
  41.9 5.3 %all_gather.9.diff = f32[4,48,128]{2,1,0:T(8,128)S(1)} all-gather(f32[1,48,128]{2,1,0:T(8,128)S(1)} %copy-done.9), channel_id=1, replica_groups=mesh['gx'=4,'gy'=8] {'gx'}, dimensions={0}, use_global_device_ids=true | all-gather | bytes 122880 | tf_op jit(solution)/shard_map/all_gather | solution.py:229
  47.3 0.9 %factors.1 = f32[288,128]{1,0:T(8,128)S(1)} custom-call(s32[4,32]{1,0:T(4,128)S(1)} %copy-done.6, f32[4,48,128]{2,1,0:T(8,128)S(1)} %all_gather.9.diff, f32[4,48,128]{2,1,0:T(8,128)S(1)} %all_gather.10.fall, f32[4,48,128]{2,1,0:T(8,128)S(1)} %all_gather.11.cloud), custom_call_target="tpu_custom_call" | custom-call | tf_op jit(solution)/shard_map/factors/pallas_call | solution.py:231
  48.2 1.5 %third.1 = f32[128,528]{1,0:T(8,128)} custom-call(f32[128,528]{1,0:T(8,128)S(1)} %bitcast.3, f32[1,528]{1,0:T(1,128)S(1)} %reshape.10.hyper, f32[128,528]{1,0:T(8,128)S(1)} %get-tuple-element.32.total, f32[4,32]{1,0:T(4,128)S(1)} %copy-done.5, f32[288,128]{1,0:T(8,128)S(1)} %factors.1, f32[32,528]{1,0:T(8,128)S(1)} %collective-permute-done.8.refs_0_, ...), custom_call_target="tpu_custom_call" | custom-call | tf_op jit(solution)/shard_map/third/pallas_call | solution.py:259
  (30 shorter events, 0.1 us)
Async XLA Ops:
  0.0 1.0 %copy-start = (f32[4,32,528]{2,1,0:T(8,128)S(1)}, f32[4,32,528]{2,1,0:T(8,128)}, u32[]{:S(2)}) copy-start(f32[4,32,528]{2,1,0:T(8,128)} %param.9) | copy-start | bytes 811012
  1.0 0.9 %copy-start.2 = (f32[2,128,128]{2,1,0:T(8,128)S(1)}, f32[2,128,128]{2,1,0:T(8,128)}, u32[]{:S(2)}) copy-start(f32[2,128,128]{2,1,0:T(8,128)} %constant.2.clone.tables) | copy-start | bytes 393220
  1.9 0.7 %copy-start.4 = (f32[4,32]{1,0:T(4,128)S(1)}, f32[4,32]{1,0:T(4,128)}, u32[]{:S(2)}) copy-start(f32[4,32]{1,0:T(4,128)} %mass.3) | copy-start | bytes 1540
  2.6 14.9 %copy-start.7 = (f32[1,48,128]{2,1,0:T(8,128)S(1)}, f32[1,48,128]{2,1,0:T(8,128)}, u32[]{:S(2)}) copy-start(f32[1,48,128]{2,1,0:T(8,128)} %param.15) | copy-start | bytes 73732
  3.0 20.3 %copy-start.3 = (f32[2,128,128]{2,1,0:T(8,128)S(1)}, f32[2,128,128]{2,1,0:T(8,128)}, u32[]{:S(2)}) copy-start(f32[2,128,128]{2,1,0:T(8,128)} %constant.2.clone.tables) | copy-start | bytes 393220
  3.0 20.2 %collective-permute-start = (f32[32,528]{1,0:T(8,128)S(1)}, f32[32,528]{1,0:T(8,128)S(1)}, u32[]{:S(2)}, u32[]{:S(2)}) collective-permute-start(f32[32,528]{1,0:T(8,128)S(1)} %get-tuple-element.24), channel_id=1, source_target_pairs={{0,8},{1,9},{2,10},{3,11},{4,12},{5,13},{6,14},{7,15},{8,16},{9,17... | collective-permute-start | bytes 202760 | tf_op jit(solution)/shard_map/ppermute | solution.py:198
  3.5 19.7 %collective-permute-start.1 = (f32[32,528]{1,0:T(8,128)S(1)}, f32[32,528]{1,0:T(8,128)S(1)}, u32[]{:S(2)}, u32[]{:S(2)}) collective-permute-start(f32[32,528]{1,0:T(8,128)S(1)} %get-tuple-element.25), channel_id=1, source_target_pairs={{0,24},{1,25},{2,26},{3,27},{4,28},{5,29},{6,30},{7,31},{8,0},{9,1... | collective-permute-start | bytes 202760 | tf_op jit(solution)/shard_map/ppermute | solution.py:198
  5.5 6.6 %collective-permute-start.4 = (f32[1,528]{1,0:T(1,128)S(1)}, f32[1,528]{1,0:T(1,128)S(1)}, u32[]{:S(2)}, u32[]{:S(2)}) collective-permute-start(f32[1,528]{1,0:T(1,128)S(1)} %get-tuple-element.28), channel_id=1, source_target_pairs={{0,9},{1,10},{2,11},{3,12},{4,13},{5,14},{6,15},{7,8},{8,17},{9,18... | collective-permute-start | bytes 6344 | tf_op jit(solution)/shard_map/ppermute | solution.py:198
  7.3 5.7 %collective-permute-start.5 = (f32[1,528]{1,0:T(1,128)S(1)}, f32[1,528]{1,0:T(1,128)S(1)}, u32[]{:S(2)}, u32[]{:S(2)}) collective-permute-start(f32[1,528]{1,0:T(1,128)S(1)} %get-tuple-element.29), channel_id=1, source_target_pairs={{0,15},{1,8},{2,9},{3,10},{4,11},{5,12},{6,13},{7,14},{8,23},{9,16... | collective-permute-start | bytes 6344 | tf_op jit(solution)/shard_map/ppermute | solution.py:198
  11.6 5.8 %collective-permute-start.6 = (f32[1,528]{1,0:T(1,128)S(1)}, f32[1,528]{1,0:T(1,128)S(1)}, u32[]{:S(2)}, u32[]{:S(2)}) collective-permute-start(f32[1,528]{1,0:T(1,128)S(1)} %get-tuple-element.30), channel_id=1, source_target_pairs={{0,25},{1,26},{2,27},{3,28},{4,29},{5,30},{6,31},{7,24},{8,1},{9,2... | collective-permute-start | bytes 6344 | tf_op jit(solution)/shard_map/ppermute | solution.py:198
  12.1 11.1 %collective-permute-start.2 = (f32[4,528]{1,0:T(4,128)S(1)}, f32[4,528]{1,0:T(4,128)S(1)}, u32[]{:S(2)}, u32[]{:S(2)}) collective-permute-start(f32[4,528]{1,0:T(4,128)S(1)} %get-tuple-element.26), channel_id=1, source_target_pairs={{0,1},{1,2},{2,3},{3,4},{4,5},{5,6},{6,7},{7,0},{8,9},{9,10},{10,1... | collective-permute-start | bytes 25352 | tf_op jit(solution)/shard_map/ppermute | solution.py:198
  13.0 10.3 %collective-permute-start.3 = (f32[4,528]{1,0:T(4,128)S(1)}, f32[4,528]{1,0:T(4,128)S(1)}, u32[]{:S(2)}, u32[]{:S(2)}) collective-permute-start(f32[4,528]{1,0:T(4,128)S(1)} %get-tuple-element.27), channel_id=1, source_target_pairs={{0,7},{1,0},{2,1},{3,2},{4,3},{5,4},{6,5},{7,6},{8,15},{9,8},{10,9... | collective-permute-start | bytes 25352 | tf_op jit(solution)/shard_map/ppermute | solution.py:198
  17.5 5.8 %collective-permute-start.7 = (f32[1,528]{1,0:T(1,128)S(1)}, f32[1,528]{1,0:T(1,128)S(1)}, u32[]{:S(2)}, u32[]{:S(2)}) collective-permute-start(f32[1,528]{1,0:T(1,128)S(1)} %get-tuple-element.31), channel_id=1, source_target_pairs={{0,31},{1,24},{2,25},{3,26},{4,27},{5,28},{6,29},{7,30},{8,7},{9,0... | collective-permute-start | bytes 6344 | tf_op jit(solution)/shard_map/ppermute | solution.py:198
  17.5 5.8 %copy-start.5 = (f32[4,32]{1,0:T(4,128)S(1)}, f32[4,32]{1,0:T(4,128)}, u32[]{:S(2)}) copy-start(f32[4,32]{1,0:T(4,128)} %inverse.3) | copy-start | bytes 1540
  23.3 7.6 %copy-start.8 = (f32[1,48,128]{2,1,0:T(8,128)S(1)}, f32[1,48,128]{2,1,0:T(8,128)}, u32[]{:S(2)}) copy-start(f32[1,48,128]{2,1,0:T(8,128)} %param.16) | copy-start | bytes 73732
  23.3 23.9 %copy-start.10 = (f32[528]{0:T(1024)S(1)}, f32[528]{0:T(1024)}, u32[]{:S(2)}) copy-start(f32[528]{0:T(1024)} %param.10) | copy-start | bytes 6340
  23.3 23.9 %copy-start.6 = (s32[4,32]{1,0:T(4,128)S(1)}, s32[4,32]{1,0:T(4,128)}, u32[]{:S(2)}) copy-start(s32[4,32]{1,0:T(4,128)} %slots.1) | copy-start | bytes 1540
  23.8 24.4 %collective-permute-start.8 = (f32[32,528]{1,0:T(8,128)S(1)}, f32[32,528]{1,0:T(8,128)S(1)}, u32[]{:S(2)}, u32[]{:S(2)}) collective-permute-start(f32[32,528]{1,0:T(8,128)S(1)} %get-tuple-element.33), channel_id=1, source_target_pairs={{0,8},{1,9},{2,10},{3,11},{4,12},{5,13},{6,14},{7,15},{8,16},{9,17... | collective-permute-start | bytes 202760 | tf_op jit(solution)/shard_map/ppermute | solution.py:198
  24.2 24.0 %collective-permute-start.9 = (f32[32,528]{1,0:T(8,128)S(1)}, f32[32,528]{1,0:T(8,128)S(1)}, u32[]{:S(2)}, u32[]{:S(2)}) collective-permute-start(f32[32,528]{1,0:T(8,128)S(1)} %get-tuple-element.34), channel_id=1, source_target_pairs={{0,24},{1,25},{2,26},{3,27},{4,28},{5,29},{6,30},{7,31},{8,0},{9,1... | collective-permute-start | bytes 202760 | tf_op jit(solution)/shard_map/ppermute | solution.py:198
  25.6 10.7 %collective-permute-start.12 = (f32[1,528]{1,0:T(1,128)S(1)}, f32[1,528]{1,0:T(1,128)S(1)}, u32[]{:S(2)}, u32[]{:S(2)}) collective-permute-start(f32[1,528]{1,0:T(1,128)S(1)} %get-tuple-element.37), channel_id=1, source_target_pairs={{0,9},{1,10},{2,11},{3,12},{4,13},{5,14},{6,15},{7,8},{8,17},{9,18... | collective-permute-start | bytes 6344 | tf_op jit(solution)/shard_map/ppermute | solution.py:198
  27.4 9.4 %collective-permute-start.13 = (f32[1,528]{1,0:T(1,128)S(1)}, f32[1,528]{1,0:T(1,128)S(1)}, u32[]{:S(2)}, u32[]{:S(2)}) collective-permute-start(f32[1,528]{1,0:T(1,128)S(1)} %get-tuple-element.38), channel_id=1, source_target_pairs={{0,15},{1,8},{2,9},{3,10},{4,11},{5,12},{6,13},{7,14},{8,23},{9,16... | collective-permute-start | bytes 6344 | tf_op jit(solution)/shard_map/ppermute | solution.py:198
  30.8 11.1 %copy-start.9 = (f32[1,48,128]{2,1,0:T(8,128)S(1)}, f32[1,48,128]{2,1,0:T(8,128)}, u32[]{:S(2)}) copy-start(f32[1,48,128]{2,1,0:T(8,128)} %param.14) | copy-start | bytes 73732
  30.8 17.4 %copy-start.1 = (f32[4,32,528]{2,1,0:T(8,128)S(1)}, f32[4,32,528]{2,1,0:T(8,128)}, u32[]{:S(2)}) copy-start(f32[4,32,528]{2,1,0:T(8,128)} %param.9) | copy-start | bytes 811012
  30.8 10.2 %collective-permute-start.14 = (f32[1,528]{1,0:T(1,128)S(1)}, f32[1,528]{1,0:T(1,128)S(1)}, u32[]{:S(2)}, u32[]{:S(2)}) collective-permute-start(f32[1,528]{1,0:T(1,128)S(1)} %get-tuple-element.39), channel_id=1, source_target_pairs={{0,25},{1,26},{2,27},{3,28},{4,29},{5,30},{6,31},{7,24},{8,1},{9,2... | collective-permute-start | bytes 6344 | tf_op jit(solution)/shard_map/ppermute | solution.py:198
  36.3 11.9 %collective-permute-start.10 = (f32[4,528]{1,0:T(4,128)S(1)}, f32[4,528]{1,0:T(4,128)S(1)}, u32[]{:S(2)}, u32[]{:S(2)}) collective-permute-start(f32[4,528]{1,0:T(4,128)S(1)} %get-tuple-element.35), channel_id=1, source_target_pairs={{0,1},{1,2},{2,3},{3,4},{4,5},{5,6},{6,7},{7,0},{8,9},{9,10},{10,1... | collective-permute-start | bytes 25352 | tf_op jit(solution)/shard_map/ppermute | solution.py:198
  36.8 11.4 %collective-permute-start.11 = (f32[4,528]{1,0:T(4,128)S(1)}, f32[4,528]{1,0:T(4,128)S(1)}, u32[]{:S(2)}, u32[]{:S(2)}) collective-permute-start(f32[4,528]{1,0:T(4,128)S(1)} %get-tuple-element.36), channel_id=1, source_target_pairs={{0,7},{1,0},{2,1},{3,2},{4,3},{5,4},{6,5},{7,6},{8,15},{9,8},{10,9... | collective-permute-start | bytes 25352 | tf_op jit(solution)/shard_map/ppermute | solution.py:198
  41.1 7.1 %collective-permute-start.15 = (f32[1,528]{1,0:T(1,128)S(1)}, f32[1,528]{1,0:T(1,128)S(1)}, u32[]{:S(2)}, u32[]{:S(2)}) collective-permute-start(f32[1,528]{1,0:T(1,128)S(1)} %get-tuple-element.40), channel_id=1, source_target_pairs={{0,31},{1,24},{2,25},{3,26},{4,27},{5,28},{6,29},{7,30},{8,7},{9,0... | collective-permute-start | bytes 6344 | tf_op jit(solution)/shard_map/ppermute | solution.py:198

commit v2 on v1

v2 whole, which is shorter than its diff:
```python
import functools

import jax
import jax.numpy as jnp
import numpy as np
from jax import lax
from jax.experimental import pallas as pl
from jax.experimental.pallas import tpu as pltpu
from jax.sharding import PartitionSpec as P

VMEM = pl.BlockSpec(memory_space=pltpu.VMEM)
PARAMS = pltpu.CompilerParams(vmem_limit_bytes=16 * 1024 * 1024)


def second_table():
    nodes = np.array([-1.0, -1.0 / np.sqrt(5.0), 1.0 / np.sqrt(5.0), 1.0])
    deriv = np.zeros((4, 4))
    for i in range(4):
        for j in range(4):
            if i == j:
                deriv[i, j] = sum(1.0 / (nodes[i] - nodes[k]) for k in range(4) if k != i)
            else:
                upper = np.prod([nodes[i] - nodes[k] for k in range(4) if k != i])
                lower = np.prod([nodes[j] - nodes[k] for k in range(4) if k != j])
                deriv[i, j] = upper / (lower * (nodes[i] - nodes[j]))
    return deriv @ deriv


def laplacian_tables(size_x, rows, columns):
    second = second_table()
    count = len(columns)
    lap = np.kron(np.kron(np.eye(size_x // 4), second), np.eye(count))
    lap = lap + np.kron(np.eye(size_x), np.kron(np.eye(count // 4), second))
    lap = lap.reshape(size_x, count, size_x * count)
    own = [columns.index(y) for y in rows]
    partner = np.zeros((size_x, len(rows), size_x * count))
    for i, y in enumerate(rows):
        other = y - 1 if y % 4 == 0 else y + 1 if y % 4 == 3 else None
        if other in columns:
            partner[:, i] = lap[:, columns.index(other)]
    both = np.stack([lap[:, own], partner])
    return both.reshape(2, size_x * len(rows), size_x * count).astype(np.float32)


def split(value):
    high = value.astype(jnp.bfloat16)
    return high, (value - high.astype(jnp.float32)).astype(jnp.bfloat16)


def product(left, right):
    left_high, left_low = left
    right_high, right_low = right
    dot = functools.partial(jnp.dot, preferred_element_type=jnp.float32)
    return dot(left_high, right_high) + (dot(left_high, right_low) + dot(left_low, right_high))


def to_column(planes, low, count, partner=False):
    size_x, size_y = planes[0][0].shape
    row = lax.broadcasted_iota(jnp.int32, (count, size_y), 0) + low
    lane = lax.broadcasted_iota(jnp.int32, (count, size_y), 1)
    if partner:
        phase = (row + 4 * count) % 4
        row = jnp.where(phase == 0, row - 1, jnp.where(phase == 3, row + 1, 4 * size_y))
    parts = []
    for x in range(size_x):
        picked = jnp.zeros((count, size_y), jnp.float32)
        for plane, first in planes:
            picked = picked + jnp.where(row == lane + first, plane[x : x + 1, :], 0.0)
        parts.append(jnp.sum(picked, axis=1, keepdims=True))
    return jnp.concatenate(parts, axis=0)


def mass_planes(own, halo_low, halo_high, which):
    size_x, size_y = own.shape
    rows = slice(which * size_x, (which + 1) * size_x)
    return (
        (own[...], 0),
        (halo_low[size_x, rows, :size_y], -size_y),
        (halo_high[size_x, rows, :size_y], size_y),
    )


def operator(tables, planes, low, count):
    mass = to_column(planes, low, count)
    partner = to_column(planes, low, count, True)
    return split(mass * tables[0] + partner * tables[1])


def pack_kernel(
    state, mass, inverse, diff, fall, cloud, low, high, coefs, mass_here, inverse_here, sems
):
    size_x, size_y, _ = state.shape
    levels = diff.shape[1]
    depth = low.shape[1]
    pairs = [
        (mass, mass_here),
        (inverse, inverse_here),
        (state.at[:, :depth, :], low.at[:size_x]),
        (state.at[:, size_y - depth :, :], high.at[:size_x]),
    ]
    for i, source in enumerate((diff, fall, cloud)):
        pairs.append((source.at[0], coefs.at[i * levels : (i + 1) * levels]))
    copies = [
        pltpu.make_async_copy(source, target, sems.at[i])
        for i, (source, target) in enumerate(pairs)
    ]
    for copy in copies:
        copy.start()
    for message in (low, high):
        message[size_x] = jnp.zeros(message.shape[1:], jnp.float32)
    copies[0].wait()
    copies[1].wait()
    for message in (low, high):
        message[size_x, :size_x, :size_y] = mass_here[...]
        message[size_x, size_x : 2 * size_x, :size_y] = inverse_here[...]
    for copy in copies[2:]:
        copy.wait()


def first_kernel(state, mass, halo_low, halo_high, tables, total, x_low, x_high, work):
    size_x, size_y, _ = state.shape
    depth = halo_low.shape[1]
    count = size_y + 2 * depth
    for x in range(size_x):
        start = x * count
        work[start : start + depth] = halo_low[x]
        work[start + depth : start + depth + size_y] = state[x]
        work[start + depth + size_y : start + count] = halo_high[x]
    planes = mass_planes(mass, halo_low, halo_high, 0)
    rows = size_y + depth
    result = product(operator(tables, planes, -depth // 2, rows), split(work[...]))
    total[...] = result
    x_low[...] = result[:rows]
    x_high[...] = result[-rows:]


def second_kernel(
    total, mass, inverse, halo_low, halo_high, tables, from_low, from_high, out, x_low, x_high, work
):
    size_x, size_y = mass.shape
    depth = halo_low.shape[1]
    rows = size_y + depth
    work[...] = total[...]
    work[:rows] += from_low[...]
    work[-rows:] += from_high[...]
    inverses = mass_planes(inverse, halo_low, halo_high, 1)
    once = to_column(inverses, -depth // 2, rows) * work[...]
    planes = mass_planes(mass, halo_low, halo_high, 0)
    result = product(operator(tables, planes, 0, size_y), split(once))
    out[...] = result
    x_low[...] = result[:size_y]
    x_high[...] = result[-size_y:]


def third_kernel(
    levels, state, hyper, total, inverse, factors, from_low, from_high, out, work, turned, values
):
    columns, width = total.shape
    size_x, size_y = inverse.shape
    variables = width // levels
    work[...] = total[...]
    work[:size_y] += from_low[...]
    work[-size_y:] += from_high[...]
    twice = to_column([(inverse[...], 0)], 0, size_y) * work[...]
    turned[...] = (state[...].reshape(columns, width) - hyper[...] * twice).T
    scale, down, up, keep, flow, cloud = (
        factors.at[i * levels : (i + 1) * levels] for i in range(6)
    )
    value = jnp.zeros((variables, columns), jnp.float32)
    for k in range(levels):
        rows = turned[pl.ds(k, variables, stride=levels), :]
        value = rows * scale[k : k + 1, :] + down[k : k + 1, :] * value
        values[k, :variables, :] = value
    solved = jnp.zeros((variables, columns), jnp.float32)
    for k in reversed(range(levels)):
        solved = values[k, :variables, :] + up[k : k + 1, :] * solved
        turned[pl.ds(k, variables, stride=levels), :] = solved
    heat, vapour, liquid = (turned.at[i * levels : (i + 1) * levels] for i in range(3))
    condensed = cloud[...] * 0.5 * jnp.maximum(vapour[...] - 0.3 * heat[...], 0.0)
    vapour[...] = vapour[...] - condensed
    heat[...] = heat[...] + 2.0 * condensed
    liquid[...] = (liquid[...] + condensed) * keep[...]
    settled = jnp.zeros((1, columns), jnp.float32)
    for k in range(levels):
        settled = liquid[k : k + 1, :] + flow[k : k + 1, :] * settled
        liquid[k : k + 1, :] = settled
    out[...] = turned[...].T.reshape(out.shape)


def factor_kernel(levels, shifts, slots, *refs):
    pieces, factors = refs[:-1], refs[-1]
    span = pieces[0].shape[-1]
    size_x, size_y = slots.shape
    columns = size_x * size_y
    peers, here = lax.axis_size("gx"), lax.axis_index("gx")
    picked = jnp.zeros((3 * levels, columns), jnp.float32)
    wanted = jnp.concatenate([slots[x : x + 1, :] for x in range(size_x)], axis=1)
    for shift, piece in zip(shifts, pieces):
        peer = lax.rem(here + peers - shift, peers)
        entry = lax.broadcasted_iota(jnp.int32, (span, columns), 0) + peer * span
        choice = (entry == wanted).astype(jnp.float32).astype(jnp.bfloat16)
        rest = piece[...]
        for _ in range(3):
            part = rest.astype(jnp.bfloat16)
            rest = rest - part.astype(jnp.float32)
            picked = picked + jnp.dot(part, choice, preferred_element_type=jnp.float32)
    mixing, falling, covered = (picked[i * levels : (i + 1) * levels] for i in range(3))
    scale, down, up, keep, flow, cover = (
        factors.at[i * levels : (i + 1) * levels] for i in range(6)
    )
    gain = jnp.zeros((1, columns), jnp.float32)
    for k in range(levels):
        above = mixing[k : k + 1] if k else jnp.zeros_like(gain)
        below = mixing[k + 1 : k + 2] if k + 1 < levels else jnp.zeros_like(gain)
        centre = 1.0 + above + (below if k + 1 < levels else mixing[:1])
        inverse = 1.0 / (centre - above * gain)
        gain = below * inverse
        scale[k : k + 1, :] = inverse
        down[k : k + 1, :] = above * inverse
        up[k : k + 1, :] = gain
    kept = 1.0 / (1.0 + falling)
    keep[...] = kept
    flow[:1, :] = jnp.zeros((1, columns), jnp.float32)
    flow[1:, :] = falling[:-1] * kept[1:]
    cover[...] = covered


def shifted(value, axis, step):
    size = lax.axis_size(axis)
    return lax.ppermute(value, axis, [(i, (i + step) % size) for i in range(size)])


def local(
    model_state, hyper_coef, point_mass, inverse_mass, span_slot, vert_diff, fall_rate, cloud_frac
):
    size_x, size_y, width = model_state.shape
    levels, span = vert_diff.shape[1:]
    columns = size_x * size_y
    depth, half = 8, 4
    rows = size_y + depth
    hyper = hyper_coef.reshape(1, width)
    wide = list(range(-depth, size_y + depth))
    middle = list(range(-half, size_y + half))
    inner = list(range(size_y))
    first_tables = jnp.asarray(laplacian_tables(size_x, middle, wide))
    second_tables = jnp.asarray(laplacian_tables(size_x, inner, middle))

    def array(*shape):
        return jax.ShapeDtypeStruct(shape, jnp.float32)

    def scratch(*shape):
        return pltpu.VMEM(shape, jnp.float32)

    def call(kernel, name, outs, scratches, *operands, spec=VMEM):
        return pl.pallas_call(
            kernel,
            out_shape=outs,
            in_specs=[spec] * len(operands),
            out_specs=[VMEM] * len(outs),
            scratch_shapes=scratches,
            compiler_params=PARAMS,
            name=name,
        )(*operands)

    edge = array(size_x + 1, depth, width)
    low, high, coefs = call(
        pack_kernel,
        "pack",
        [edge, edge, array(3 * levels, span)],
        [scratch(size_x, size_y), scratch(size_x, size_y), pltpu.SemaphoreType.DMA((7,))],
        *(
            pltpu.with_memory_space_constraint(value, pltpu.HBM)
            for value in (
                model_state,
                point_mass,
                inverse_mass,
                vert_diff,
                fall_rate,
                cloud_frac,
            )
        ),
        spec=pl.BlockSpec(memory_space=pltpu.HBM),
    )
    halo_low, halo_high = shifted(high, "gy", 1), shifted(low, "gy", -1)
    shifts = range(lax.axis_size("gx"))
    if len(shifts) <= 4:
        pieces = [coefs] + [shifted(coefs, "gx", step) for step in shifts[1:]]
    else:
        gathered = lax.all_gather(coefs, "gx")
        here = lax.axis_index("gx")
        pieces = [gathered[(here - step) % len(shifts)] for step in shifts]
    (factors,) = call(
        functools.partial(factor_kernel, levels, shifts),
        "factors",
        [array(6 * levels, columns)],
        [],
        span_slot,
        *pieces,
    )

    total, x_low, x_high = call(
        first_kernel,
        "first",
        [array(size_x * rows, width), array(rows, width), array(rows, width)],
        [scratch(size_x * len(wide), width)],
        model_state,
        point_mass,
        halo_low,
        halo_high,
        first_tables,
    )
    total, x_low, x_high = call(
        second_kernel,
        "second",
        [array(columns, width), array(size_y, width), array(size_y, width)],
        [scratch(size_x * rows, width)],
        total,
        point_mass,
        inverse_mass,
        halo_low,
        halo_high,
        second_tables,
        shifted(x_high, "gx", 1),
        shifted(x_low, "gx", -1),
    )
    (result,) = call(
        functools.partial(third_kernel, levels),
        "third",
        [array(size_x, size_y, width)],
        [scratch(columns, width), scratch(width, columns), scratch(levels, 16, columns)],
        model_state,
        hyper,
        total,
        inverse_mass,
        factors,
        shifted(x_high, "gx", 1),
        shifted(x_low, "gx", -1),
    )
    return result


def solution(mesh):
    placed = (
        P("gx", "gy", None),
        P(),
        P("gx", "gy"),
        P("gx", "gy"),
        P("gx", "gy"),
        P("gy", None, "gx"),
        P("gy", None, "gx"),
        P("gy", None, "gx"),
    )
    return jax.shard_map(
        local, mesh=mesh, in_specs=placed, out_specs=P("gx", "gy", None), check_vma=False
    )
```

time: 50 us -> 25.1 us (0.50)
  the two profiles are of different devices: /device:TPU:0 before, /device:TPU:1 now
where the time goes in v2:
time: 25.1 us; the launch traced here: 24.9 us
  starting transfers between devices  11.2 us (45%)
  waiting for transfers between devices  8.08 us (32%)
  Pallas kernels  4.48 us (18%)
  local copies, waits for them, and re-layouts  1 us (4%)
    ppermute x9, starting transfers between devices, shifted(): lax.ppermute(value, axis, [(i, (i + step) % size) for i in range(size)])  11.2 us
    ppermute x9, waiting for transfers between devices, shifted(): lax.ppermute(value, axis, [(i, (i + step) % size) for i in range(size)])  8.08 us
    pallas_call x5, Pallas kernels, call(): pl.pallas_call(kernel, out_shape=outs, in_specs=[spec] * len(operands), o...  4.48 us
    unnamed x14, local copies, waits for them, and re-layouts  1 us
  transfers between devices with their start and end apart: 9, of which 5 were waited for; matrix products, arithmetic and copies ran while one was open for 0% of the time, Pallas kernels for 5%

profile of v2, /device:TPU:1, one launch (start us, length us, event | category | flops | bytes accessed | tf_op | source)
XLA Modules:
  0.0 24.9 jit_solution(7436297572480415027)
XLA Ops:
  0.0 1.1 %pack.1 = (f32[5,8,528]{2,1,0:T(8,128)S(1)}, f32[5,8,528]{2,1,0:T(8,128)S(1)}, f32[144,128]{1,0:T(8,128)S(1)}) custom-call(f32[4,32,528]{2,1,0:T(8,128)} %state.5, f32[4,32]{1,0:T(4,128)} %mass.5, f32[4,32]{1,0:T(4,128)} %inverse.5, f32[1,48,128]{2,1,0:T(8,128)} %diff.1, f32[1,48,128]{2,1,0:T(8,128)} %fall.1, f32[1,48,128]{2,1,0:T(8,128)} %cloud.1), custom_call_target="tpu_custom_call" | custom-call | tf_op jit(solution)/shard_map/pack/pallas_call | solution.py:255
  1.1 0.0 copy-start.3
  1.1 2.1 %collective-permute-start = (f32[5,8,528]{2,1,0:T(8,128)S(1)}, f32[5,8,528]{2,1,0:T(8,128)S(1)}, u32[]{:S(2)}, u32[]{:S(2)}) collective-permute-start(f32[5,8,528]{2,1,0:T(8,128)S(1)} %get-tuple-element.14), channel_id=1, source_target_pairs={{0,1},{1,2},{2,3},{3,4},{4,5},{5,6},{6,7},{7,0},{8,9},{9,10},{10,1... | collective-permute-start | bytes 253448 | tf_op jit(solution)/shard_map/ppermute | solution.py:230
  3.2 3.1 %collective-permute-start.1 = (f32[5,8,528]{2,1,0:T(8,128)S(1)}, f32[5,8,528]{2,1,0:T(8,128)S(1)}, u32[]{:S(2)}, u32[]{:S(2)}) collective-permute-start(f32[5,8,528]{2,1,0:T(8,128)S(1)} %get-tuple-element.15), channel_id=1, source_target_pairs={{0,7},{1,0},{2,1},{3,2},{4,3},{5,4},{6,5},{7,6},{8,15},{9,8},{10,9... | collective-permute-start | bytes 253448 | tf_op jit(solution)/shard_map/ppermute | solution.py:230
  6.3 2.5 %collective-permute-done.halo_low = f32[5,8,528]{2,1,0:T(8,128)S(1)} collective-permute-done((f32[5,8,528]{2,1,0:T(8,128)S(1)}, f32[5,8,528]{2,1,0:T(8,128)S(1)}, u32[]{:S(2)}, u32[]{:S(2)}) %collective-permute-start) | collective-permute-done | bytes 84512 | tf_op jit(solution)/shard_map/ppermute | solution.py:230
  8.9 0.0 collective-permute-done.1.halo_high
  8.9 0.0 copy-done
  8.9 0.0 copy-done.3
  8.9 0.0 copy-start.1
  8.9 1.0 %copy-done.1 = f32[2,160,192]{2,1,0:T(8,128)S(1)} copy-done((f32[2,160,192]{2,1,0:T(8,128)S(1)}, f32[2,160,192]{2,1,0:T(8,128)}, u32[]{:S(2)}) %copy-start.1) | copy-done | bytes 245784
  9.9 0.5 %first.1 = (f32[160,528]{1,0:T(8,128)S(1)}, f32[40,528]{1,0:T(8,128)S(1)}, f32[40,528]{1,0:T(8,128)S(1)}) custom-call(f32[4,32,528]{2,1,0:T(8,128)S(1)} %copy-done, f32[4,32]{1,0:T(4,128)S(1)} %copy-done.3, f32[5,8,528]{2,1,0:T(8,128)S(1)} %collective-permute-done.halo_low, f32[5,8,528]{2,1,0:T(8,128)S(1)} %collective-permute-done.1.halo_high, ...), custom_call_target="tpu_custom_call" | custom-call | tf_op jit(solution)/shard_map/first/pallas_call | solution.py:255
  10.4 3.3 %collective-permute-start.2 = (f32[40,528]{1,0:T(8,128)S(1)}, f32[40,528]{1,0:T(8,128)S(1)}, u32[]{:S(2)}, u32[]{:S(2)}) collective-permute-start(f32[40,528]{1,0:T(8,128)S(1)} %get-tuple-element.17), channel_id=1, source_target_pairs={{0,8},{8,16},{16,24},{24,0},{1,9},{9,17},{17,25},{25,1},{2,10},{10... | collective-permute-start | bytes 253448 | tf_op jit(solution)/shard_map/ppermute | solution.py:230
  13.7 0.0 collective-permute-start.3
  13.7 1.7 %collective-permute-start.4 = (f32[144,128]{1,0:T(8,128)S(1)}, f32[144,128]{1,0:T(8,128)S(1)}, u32[]{:S(2)}, u32[]{:S(2)}) collective-permute-start(f32[144,128]{1,0:T(8,128)S(1)} %get-tuple-element.20.refs_0_), channel_id=1, source_target_pairs={{0,8},{8,16},{16,24},{24,0},{1,9},{9,17},{17,25},{25,1},{2,10},{10... | collective-permute-start | bytes 221192 | tf_op jit(solution)/shard_map/ppermute | solution.py:230
  15.4 0.3 %collective-permute-start.5 = (f32[144,128]{1,0:T(8,128)S(1)}, f32[144,128]{1,0:T(8,128)S(1)}, u32[]{:S(2)}, u32[]{:S(2)}) collective-permute-start(f32[144,128]{1,0:T(8,128)S(1)} %get-tuple-element.20.refs_0_), channel_id=1, source_target_pairs={{0,16},{8,24},{16,0},{24,8},{1,17},{9,25},{17,1},{25,9},{2,18},{10... | collective-permute-start | bytes 221192 | tf_op jit(solution)/shard_map/ppermute | solution.py:230
  15.7 0.2 collective-permute-start.6
  15.9 0.0 collective-permute-done.2.from_low
  15.9 3.0 %collective-permute-done.3.from_high = f32[40,528]{1,0:T(8,128)S(1)} collective-permute-done((f32[40,528]{1,0:T(8,128)S(1)}, f32[40,528]{1,0:T(8,128)S(1)}, u32[]{:S(2)}, u32[]{:S(2)}) %collective-permute-start.3) | collective-permute-done | bytes 84512 | tf_op jit(solution)/shard_map/ppermute | solution.py:230
  18.9 0.0 copy-done.2
  18.9 0.0 copy-done.4
  18.9 0.5 %second.1 = (f32[128,528]{1,0:T(8,128)S(1)}, f32[32,528]{1,0:T(8,128)S(1)}, f32[32,528]{1,0:T(8,128)S(1)}) custom-call(f32[160,528]{1,0:T(8,128)S(1)} %get-tuple-element.16.total, f32[4,32]{1,0:T(4,128)S(1)} %copy-done.3, f32[4,32]{1,0:T(4,128)S(1)} %copy-done.4, f32[5,8,528]{2,1,0:T(8,128)S(1)} %collective-permute-done.halo_low, ...), custom_call_target="tpu_custom_call" | custom-call | tf_op jit(solution)/shard_map/second/pallas_call | solution.py:255
  19.4 0.1 collective-permute-start.7
  19.4 0.0 copy-start.5
  19.4 0.5 %collective-permute-start.8 = (f32[32,528]{1,0:T(8,128)S(1)}, f32[32,528]{1,0:T(8,128)S(1)}, u32[]{:S(2)}, u32[]{:S(2)}) collective-permute-start(f32[32,528]{1,0:T(8,128)S(1)} %get-tuple-element.22), channel_id=1, source_target_pairs={{0,24},{8,0},{16,8},{24,16},{1,25},{9,1},{17,9},{25,17},{2,26},{10... | collective-permute-start | bytes 202760 | tf_op jit(solution)/shard_map/ppermute | solution.py:230
  19.9 0.0 collective-permute-done.4.refs_1_
  19.9 0.1 collective-permute-done.5.refs_2_
  20.0 1.4 %collective-permute-done.6.refs_3_ = f32[144,128]{1,0:T(8,128)S(1)} collective-permute-done((f32[144,128]{1,0:T(8,128)S(1)}, f32[144,128]{1,0:T(8,128)S(1)}, u32[]{:S(2)}, u32[]{:S(2)}) %collective-permute-start.6) | collective-permute-done | bytes 73760 | tf_op jit(solution)/shard_map/ppermute | solution.py:230
  21.4 0.0 copy-done.5
  21.4 0.9 %factors.1 = f32[288,128]{1,0:T(8,128)S(1)} custom-call(s32[4,32]{1,0:T(4,128)S(1)} %copy-done.5, f32[144,128]{1,0:T(8,128)S(1)} %get-tuple-element.20.refs_0_, f32[144,128]{1,0:T(8,128)S(1)} %collective-permute-done.4.refs_1_, f32[144,128]{1,0:T(8,128)S(1)} %collective-permute-done.5.refs_2_, f32[144,128]{1,0:T(8,128)S(1)} %collective-permute-done.6.refs_3_), custom_call_target="tpu_custom_call" | custom-call | tf_op jit(solution)/shard_map/factors/pallas_call | solution.py:255
  22.3 0.0 collective-permute-done.7.from_low
  22.3 1.0 %collective-permute-done.8.from_high = f32[32,528]{1,0:T(8,128)S(1)} collective-permute-done((f32[32,528]{1,0:T(8,128)S(1)}, f32[32,528]{1,0:T(8,128)S(1)}, u32[]{:S(2)}, u32[]{:S(2)}) %collective-permute-start.8) | collective-permute-done | bytes 67616 | tf_op jit(solution)/shard_map/ppermute | solution.py:230
  23.4 1.5 %third.1 = f32[4,32,528]{2,1,0:T(8,128)} custom-call(f32[4,32,528]{2,1,0:T(8,128)S(1)} %copy-done, f32[1,528]{1,0:T(1,128)S(1)} %reshape.3.hyper, f32[128,528]{1,0:T(8,128)S(1)} %get-tuple-element.19.total, f32[4,32]{1,0:T(4,128)S(1)} %copy-done.4, f32[288,128]{1,0:T(8,128)S(1)} %factors.1, f32[32,528]{1,0:T(8,128)S(1)} %collective-permute-done.7.from_low, ...), custom_call_target="tpu_custom_call" | custom-call | tf_op jit(solution)/shard_map/third/pallas_call | solution.py:255
  (6 shorter events, 0.0 us)
Async XLA Ops:
  0.0 8.9 %copy-start = (f32[4,32,528]{2,1,0:T(8,128)S(1)}, f32[4,32,528]{2,1,0:T(8,128)}, u32[]{:S(2)}) copy-start(f32[4,32,528]{2,1,0:T(8,128)} %state.5) | copy-start | bytes 811012
  1.1 7.8 %copy-start.3 = (f32[4,32]{1,0:T(4,128)S(1)}, f32[4,32]{1,0:T(4,128)}, u32[]{:S(2)}) copy-start(f32[4,32]{1,0:T(4,128)} %mass.5) | copy-start | bytes 1540
  1.1 7.8 %collective-permute-start = (f32[5,8,528]{2,1,0:T(8,128)S(1)}, f32[5,8,528]{2,1,0:T(8,128)S(1)}, u32[]{:S(2)}, u32[]{:S(2)}) collective-permute-start(f32[5,8,528]{2,1,0:T(8,128)S(1)} %get-tuple-element.14), channel_id=1, source_target_pairs={{0,1},{1,2},{2,3},{3,4},{4,5},{5,6},{6,7},{7,0},{8,9},{9,10},{10,1... | collective-permute-start | bytes 253448 | tf_op jit(solution)/shard_map/ppermute | solution.py:230
  3.2 5.7 %collective-permute-start.1 = (f32[5,8,528]{2,1,0:T(8,128)S(1)}, f32[5,8,528]{2,1,0:T(8,128)S(1)}, u32[]{:S(2)}, u32[]{:S(2)}) collective-permute-start(f32[5,8,528]{2,1,0:T(8,128)S(1)} %get-tuple-element.15), channel_id=1, source_target_pairs={{0,7},{1,0},{2,1},{3,2},{4,3},{5,4},{6,5},{7,6},{8,15},{9,8},{10,9... | collective-permute-start | bytes 253448 | tf_op jit(solution)/shard_map/ppermute | solution.py:230
  8.9 1.0 %copy-start.1 = (f32[2,160,192]{2,1,0:T(8,128)S(1)}, f32[2,160,192]{2,1,0:T(8,128)}, u32[]{:S(2)}) copy-start(f32[2,160,192]{2,1,0:T(8,128)} %constant.4.clone.tables) | copy-start | bytes 737284
  9.9 9.0 %copy-start.2 = (f32[2,128,160]{2,1,0:T(8,128)S(1)}, f32[2,128,160]{2,1,0:T(8,128)}, u32[]{:S(2)}) copy-start(f32[2,128,160]{2,1,0:T(8,128)} %constant.5.clone.tables) | copy-start | bytes 491524
  10.4 5.5 %collective-permute-start.2 = (f32[40,528]{1,0:T(8,128)S(1)}, f32[40,528]{1,0:T(8,128)S(1)}, u32[]{:S(2)}, u32[]{:S(2)}) collective-permute-start(f32[40,528]{1,0:T(8,128)S(1)} %get-tuple-element.17), channel_id=1, source_target_pairs={{0,8},{8,16},{16,24},{24,0},{1,9},{9,17},{17,25},{25,1},{2,10},{10... | collective-permute-start | bytes 253448 | tf_op jit(solution)/shard_map/ppermute | solution.py:230
  13.7 5.2 %copy-start.4 = (f32[4,32]{1,0:T(4,128)S(1)}, f32[4,32]{1,0:T(4,128)}, u32[]{:S(2)}) copy-start(f32[4,32]{1,0:T(4,128)} %inverse.5) | copy-start | bytes 1540
  13.7 5.2 %collective-permute-start.3 = (f32[40,528]{1,0:T(8,128)S(1)}, f32[40,528]{1,0:T(8,128)S(1)}, u32[]{:S(2)}, u32[]{:S(2)}) collective-permute-start(f32[40,528]{1,0:T(8,128)S(1)} %get-tuple-element.18), channel_id=1, source_target_pairs={{0,24},{8,0},{16,8},{24,16},{1,25},{9,1},{17,9},{25,17},{2,26},{10... | collective-permute-start | bytes 253448 | tf_op jit(solution)/shard_map/ppermute | solution.py:230
  13.7 6.3 %collective-permute-start.4 = (f32[144,128]{1,0:T(8,128)S(1)}, f32[144,128]{1,0:T(8,128)S(1)}, u32[]{:S(2)}, u32[]{:S(2)}) collective-permute-start(f32[144,128]{1,0:T(8,128)S(1)} %get-tuple-element.20.refs_0_), channel_id=1, source_target_pairs={{0,8},{8,16},{16,24},{24,0},{1,9},{9,17},{17,25},{25,1},{2,10},{10... | collective-permute-start | bytes 221192 | tf_op jit(solution)/shard_map/ppermute | solution.py:230
  15.4 4.6 %collective-permute-start.5 = (f32[144,128]{1,0:T(8,128)S(1)}, f32[144,128]{1,0:T(8,128)S(1)}, u32[]{:S(2)}, u32[]{:S(2)}) collective-permute-start(f32[144,128]{1,0:T(8,128)S(1)} %get-tuple-element.20.refs_0_), channel_id=1, source_target_pairs={{0,16},{8,24},{16,0},{24,8},{1,17},{9,25},{17,1},{25,9},{2,18},{10... | collective-permute-start | bytes 221192 | tf_op jit(solution)/shard_map/ppermute | solution.py:230
  15.7 5.8 %collective-permute-start.6 = (f32[144,128]{1,0:T(8,128)S(1)}, f32[144,128]{1,0:T(8,128)S(1)}, u32[]{:S(2)}, u32[]{:S(2)}) collective-permute-start(f32[144,128]{1,0:T(8,128)S(1)} %get-tuple-element.20.refs_0_), channel_id=1, source_target_pairs={{0,24},{8,0},{16,8},{24,16},{1,25},{9,1},{17,9},{25,17},{2,26},{10... | collective-permute-start | bytes 221192 | tf_op jit(solution)/shard_map/ppermute | solution.py:230
  18.9 1.1 %copy-start.6 = (f32[528]{0:T(1024)S(1)}, f32[528]{0:T(1024)}, u32[]{:S(2)}) copy-start(f32[528]{0:T(1024)} %param.11) | copy-start | bytes 6340
  19.4 3.0 %collective-permute-start.7 = (f32[32,528]{1,0:T(8,128)S(1)}, f32[32,528]{1,0:T(8,128)S(1)}, u32[]{:S(2)}, u32[]{:S(2)}) collective-permute-start(f32[32,528]{1,0:T(8,128)S(1)} %get-tuple-element.21), channel_id=1, source_target_pairs={{0,8},{8,16},{16,24},{24,0},{1,9},{9,17},{17,25},{25,1},{2,10},{10... | collective-permute-start | bytes 202760 | tf_op jit(solution)/shard_map/ppermute | solution.py:230
  19.4 2.0 %copy-start.5 = (s32[4,32]{1,0:T(4,128)S(1)}, s32[4,32]{1,0:T(4,128)}, u32[]{:S(2)}) copy-start(s32[4,32]{1,0:T(4,128)} %slots.1) | copy-start | bytes 1540
  19.4 3.9 %collective-permute-start.8 = (f32[32,528]{1,0:T(8,128)S(1)}, f32[32,528]{1,0:T(8,128)S(1)}, u32[]{:S(2)}, u32[]{:S(2)}) collective-permute-start(f32[32,528]{1,0:T(8,128)S(1)} %get-tuple-element.22), channel_id=1, source_target_pairs={{0,24},{8,0},{16,8},{24,16},{1,25},{9,1},{17,9},{25,17},{2,26},{10... | collective-permute-start | bytes 202760 | tf_op jit(solution)/shard_map/ppermute | solution.py:230

commit v3 on v2

v3 whole, which is shorter than its diff:
```python
import functools

import jax
import jax.numpy as jnp
import numpy as np
from jax import lax
from jax.experimental import pallas as pl
from jax.experimental.pallas import tpu as pltpu
from jax.sharding import PartitionSpec as P

VMEM = pl.BlockSpec(memory_space=pltpu.VMEM)
PARAMS = pltpu.CompilerParams(vmem_limit_bytes=16 * 1024 * 1024)


def second_table():
    nodes = np.array([-1.0, -1.0 / np.sqrt(5.0), 1.0 / np.sqrt(5.0), 1.0])
    deriv = np.zeros((4, 4))
    for i in range(4):
        for j in range(4):
            if i == j:
                deriv[i, j] = sum(1.0 / (nodes[i] - nodes[k]) for k in range(4) if k != i)
            else:
                upper = np.prod([nodes[i] - nodes[k] for k in range(4) if k != i])
                lower = np.prod([nodes[j] - nodes[k] for k in range(4) if k != j])
                deriv[i, j] = upper / (lower * (nodes[i] - nodes[j]))
    return deriv @ deriv


def laplacian_tables(size_x, size_y):
    second = second_table()
    lap = np.kron(np.kron(np.eye(size_x // 4), second), np.eye(size_y))
    lap = lap + np.kron(np.eye(size_x), np.kron(np.eye(size_y // 4), second))
    partner = np.zeros_like(lap)
    for x in range(size_x):
        for y in range(size_y):
            other = y - 1 if y % 4 == 0 else y + 1 if y % 4 == 3 else -1
            if 0 <= other < size_y:
                partner[x * size_y + y] = lap[x * size_y + other]
    return np.stack([lap, partner]).astype(np.float32)


def split(value):
    high = value.astype(jnp.bfloat16)
    return high, (value - high.astype(jnp.float32)).astype(jnp.bfloat16)


def product(left, right):
    left_high, left_low = left
    right_high, right_low = right
    dot = functools.partial(jnp.dot, preferred_element_type=jnp.float32)
    return dot(left_high, right_high) + (dot(left_high, right_low) + dot(left_low, right_high))


def to_column(plane, partner=False):
    size_x, size_y = plane.shape
    row = lax.broadcasted_iota(jnp.int32, (size_y, size_y), 0)
    lane = lax.broadcasted_iota(jnp.int32, (size_y, size_y), 1)
    if partner:
        row = jnp.where(row % 4 == 0, row - 1, jnp.where(row % 4 == 3, row + 1, -1))
    pick = row == lane
    parts = [
        jnp.sum(jnp.where(pick, plane[x : x + 1, :], 0.0), axis=1, keepdims=True)
        for x in range(size_x)
    ]
    return jnp.concatenate(parts, axis=0)


def start_kernel(
    state,
    mass,
    inverse,
    diff,
    fall,
    cloud,
    tables,
    here,
    total,
    x_low,
    x_high,
    operator,
    columns,
    coefs,
    mass_here,
    inverse_here,
    tables_here,
    sems,
):
    size_x, size_y, width = state.shape
    levels = diff.shape[1]
    pairs = [(mass, mass_here), (tables, tables_here), (inverse, inverse_here), (state, here)]
    for i, source in enumerate((diff, fall, cloud)):
        pairs.append((source.at[0], coefs.at[i * levels : (i + 1) * levels]))
    copies = [
        pltpu.make_async_copy(source, target, sems.at[i])
        for i, (source, target) in enumerate(pairs)
    ]
    for copy in copies:
        copy.start()
    for copy in copies[:3]:
        copy.wait()
    own = to_column(mass_here[...])
    lane = lax.broadcasted_iota(jnp.int32, columns.shape, 1)
    columns[...] = jnp.where(lane == 0, own, to_column(inverse_here[...]))
    matrix = own * tables_here[0] + to_column(mass_here[...], True) * tables_here[1]
    operator[...] = matrix
    copies[3].wait()
    result = product(split(matrix), split(here[...].reshape(size_x * size_y, width)))
    total[...] = result
    x_low[...] = result[:size_y]
    x_high[...] = result[-size_y:]
    for copy in copies[4:]:
        copy.wait()


def edge_rows(ref, y, size_x, size_y):
    return jnp.concatenate(
        [ref[x * size_y + y : x * size_y + y + 1, :] for x in range(size_x)], axis=0
    )


def turn_kernel(size_x, total, columns, operator, from_low, from_high, out, y_low, y_high):
    size_y = from_low.shape[0]
    width = total.shape[1]
    out[...] = total[...]
    out[:size_y] += from_low[...]
    out[-size_y:] += from_high[...]
    once = split(columns[:, 1:2] * out[...])
    for y, message in ((0, y_low), (size_y - 1, y_high)):
        rows = product(split(edge_rows(operator, y, size_x, size_y)), once)
        message[:size_x, :width] = edge_rows(out, y, size_x, size_y)
        message[size_x:, :width] = rows
        message[:size_x, width : width + 2] = edge_rows(columns, y, size_x, size_y)[:, :2]


def second_kernel(
    size_x, known, columns, operator, from_low, from_high, out, x_low, x_high, work
):
    size_y = x_low.shape[0]
    width = known.shape[1]
    second = second_table()
    work[...] = known[...]
    beyond = []
    for y, node, message in ((0, 3, from_low), (size_y - 1, 0, from_high)):
        mass = message[:size_x, width : width + 1]
        inverse = message[:size_x, width + 1 : width + 2]
        theirs = inverse * edge_rows(known, y, size_x, size_y)
        rows = []
        for x in range(size_x):
            row = message[size_x + x : size_x + x + 1, :width]
            line = sum(
                float(second[x, i] + second[node, node] * (x == i)) * theirs[i : i + 1]
                for i in range(size_x)
            )
            rows.append(row + mass[x : x + 1] * line)
            work[x * size_y + y : x * size_y + y + 1, :] += message[x : x + 1, :width]
        beyond.append(rows)
    result = product(split(operator[...]), split(columns[:, 1:2] * work[...]))
    out[...] = result
    for y, rows in zip((0, size_y - 1), beyond):
        for x in range(size_x):
            out[x * size_y + y : x * size_y + y + 1, :] += rows[x]
    x_low[...] = out[:size_y]
    x_high[...] = out[-size_y:]


def third_kernel(
    levels, state, hyper, total, masses, factors, from_low, from_high, out, work, turned, values
):
    columns, width = total.shape
    size_x, size_y, _ = state.shape
    variables = width // levels
    work[...] = total[...]
    work[:size_y] += from_low[...]
    work[-size_y:] += from_high[...]
    twice = masses[:, 1:2] * work[...]
    turned[...] = (state[...].reshape(columns, width) - hyper[...] * twice).T
    scale, down, up, keep, flow, cloud = (
        factors.at[i * levels : (i + 1) * levels] for i in range(6)
    )
    value = jnp.zeros((variables, columns), jnp.float32)
    for k in range(levels):
        rows = turned[pl.ds(k, variables, stride=levels), :]
        value = rows * scale[k : k + 1, :] + down[k : k + 1, :] * value
        values[k, :variables, :] = value
    solved = jnp.zeros((variables, columns), jnp.float32)
    for k in reversed(range(levels)):
        solved = values[k, :variables, :] + up[k : k + 1, :] * solved
        turned[pl.ds(k, variables, stride=levels), :] = solved
    heat, vapour, liquid = (turned.at[i * levels : (i + 1) * levels] for i in range(3))
    condensed = cloud[...] * 0.5 * jnp.maximum(vapour[...] - 0.3 * heat[...], 0.0)
    vapour[...] = vapour[...] - condensed
    heat[...] = heat[...] + 2.0 * condensed
    liquid[...] = (liquid[...] + condensed) * keep[...]
    settled = jnp.zeros((1, columns), jnp.float32)
    for k in range(levels):
        settled = liquid[k : k + 1, :] + flow[k : k + 1, :] * settled
        liquid[k : k + 1, :] = settled
    out[...] = turned[...].T.reshape(out.shape)


def factor_kernel(levels, shifts, slots, *refs):
    pieces, factors = refs[:-1], refs[-1]
    span = pieces[0].shape[-1]
    size_x, size_y = slots.shape
    columns = size_x * size_y
    peers, here = lax.axis_size("gx"), lax.axis_index("gx")
    picked = jnp.zeros((3 * levels, columns), jnp.float32)
    wanted = jnp.concatenate([slots[x : x + 1, :] for x in range(size_x)], axis=1)
    for shift, piece in zip(shifts, pieces):
        peer = lax.rem(here + peers - shift, peers)
        entry = lax.broadcasted_iota(jnp.int32, (span, columns), 0) + peer * span
        choice = (entry == wanted).astype(jnp.float32).astype(jnp.bfloat16)
        rest = piece[...]
        for _ in range(3):
            part = rest.astype(jnp.bfloat16)
            rest = rest - part.astype(jnp.float32)
            picked = picked + jnp.dot(part, choice, preferred_element_type=jnp.float32)
    mixing, falling, covered = (picked[i * levels : (i + 1) * levels] for i in range(3))
    scale, down, up, keep, flow, cover = (
        factors.at[i * levels : (i + 1) * levels] for i in range(6)
    )
    gain = jnp.zeros((1, columns), jnp.float32)
    for k in range(levels):
        above = mixing[k : k + 1] if k else jnp.zeros_like(gain)
        below = mixing[k + 1 : k + 2] if k + 1 < levels else jnp.zeros_like(gain)
        centre = 1.0 + above + (below if k + 1 < levels else mixing[:1])
        inverse = 1.0 / (centre - above * gain)
        gain = below * inverse
        scale[k : k + 1, :] = inverse
        down[k : k + 1, :] = above * inverse
        up[k : k + 1, :] = gain
    kept = 1.0 / (1.0 + falling)
    keep[...] = kept
    flow[:1, :] = jnp.zeros((1, columns), jnp.float32)
    flow[1:, :] = falling[:-1] * kept[1:]
    cover[...] = covered


def shifted(value, axis, step):
    size = lax.axis_size(axis)
    return lax.ppermute(value, axis, [(i, (i + step) % size) for i in range(size)])


def local(
    model_state, hyper_coef, point_mass, inverse_mass, span_slot, vert_diff, fall_rate, cloud_frac
):
    size_x, size_y, width = model_state.shape
    levels, span = vert_diff.shape[1:]
    columns = size_x * size_y
    hyper = hyper_coef.reshape(1, width)
    padded = -(-(width + 2) // 128) * 128
    tables = jnp.asarray(laplacian_tables(size_x, size_y))

    def array(*shape):
        return jax.ShapeDtypeStruct(shape, jnp.float32)

    def scratch(*shape):
        return pltpu.VMEM(shape, jnp.float32)

    def call(kernel, name, outs, scratches, *operands, spec=VMEM):
        return pl.pallas_call(
            kernel,
            out_shape=outs,
            in_specs=[spec] * len(operands),
            out_specs=[VMEM] * len(outs),
            scratch_shapes=scratches,
            compiler_params=PARAMS,
            name=name,
        )(*operands)

    whole, line, edge = array(columns, width), array(size_y, width), array(2 * size_x, padded)
    here, total, x_low, x_high, operator, masses, coefs = call(
        start_kernel,
        "start",
        [
            array(size_x, size_y, width),
            whole,
            line,
            line,
            array(columns, columns),
            array(columns, 128),
            array(3 * levels, span),
        ],
        [
            scratch(size_x, size_y),
            scratch(size_x, size_y),
            scratch(*tables.shape),
            pltpu.SemaphoreType.DMA((7,)),
        ],
        *(
            pltpu.with_memory_space_constraint(value, pltpu.HBM)
            for value in (
                model_state,
                point_mass,
                inverse_mass,
                vert_diff,
                fall_rate,
                cloud_frac,
                tables,
            )
        ),
        spec=pl.BlockSpec(memory_space=pltpu.HBM),
    )
    known, y_low, y_high = call(
        functools.partial(turn_kernel, size_x),
        "turn",
        [whole, edge, edge],
        [],
        total,
        masses,
        operator,
        shifted(x_high, "gx", 1),
        shifted(x_low, "gx", -1),
    )
    total, x_low, x_high = call(
        functools.partial(second_kernel, size_x),
        "second",
        [whole, line, line],
        [scratch(columns, width)],
        known,
        masses,
        operator,
        shifted(y_high, "gy", 1),
        shifted(y_low, "gy", -1),
    )
    coefs, _ = lax.optimization_barrier((coefs, y_low))
    shifts = range(lax.axis_size("gx"))
    if len(shifts) <= 4:
        pieces = [coefs] + [shifted(coefs, "gx", step) for step in shifts[1:]]
    else:
        gathered = lax.all_gather(coefs, "gx")
        place = lax.axis_index("gx")
        pieces = [gathered[(place - step) % len(shifts)] for step in shifts]
    (factors,) = call(
        functools.partial(factor_kernel, levels, shifts),
        "factors",
        [array(6 * levels, columns)],
        [],
        span_slot,
        *pieces,
    )

    (result,) = call(
        functools.partial(third_kernel, levels),
        "third",
        [array(size_x, size_y, width)],
        [scratch(columns, width), scratch(width, columns), scratch(levels, 16, columns)],
        here,
        hyper,
        total,
        masses,
        factors,
        shifted(x_high, "gx", 1),
        shifted(x_low, "gx", -1),
    )
    return result


def solution(mesh):
    placed = (
        P("gx", "gy", None),
        P(),
        P("gx", "gy"),
        P("gx", "gy"),
        P("gx", "gy"),
        P("gy", None, "gx"),
        P("gy", None, "gx"),
        P("gy", None, "gx"),
    )
    return jax.shard_map(
        local, mesh=mesh, in_specs=placed, out_specs=P("gx", "gy", None), check_vma=False
    )
```

time: 25.1 us -> 21.6 us (0.86)
  the two profiles are of different devices: /device:TPU:1 before, /device:TPU:0 now
where the time goes in v3:
time: 21.6 us; the launch traced here: 21.3 us
  starting transfers between devices  12 us (56%)
  waiting for transfers between devices  4.64 us (21%)
  Pallas kernels  4.54 us (21%)
    ppermute x9, starting transfers between devices, shifted(): lax.ppermute(value, axis, [(i, (i + step) % size) for i in range(size)])  12 us
    ppermute x9, waiting for transfers between devices, shifted(): lax.ppermute(value, axis, [(i, (i + step) % size) for i in range(size)])  4.64 us
    pallas_call x5, Pallas kernels, call(): pl.pallas_call(kernel, out_shape=outs, in_specs=[spec] * len(operands), o...  4.54 us
  transfers between devices with their start and end apart: 9, of which 4 were waited for; matrix products, arithmetic and copies ran while one was open for 0% of the time, Pallas kernels for 6%

profile of v3, /device:TPU:0, one launch (start us, length us, event | category | flops | bytes accessed | tf_op | source)
XLA Modules:
  0.0 21.3 jit_solution(17921324493518273536)
XLA Ops:
  0.0 1.5 %start.1 = (f32[4,32,528]{2,1,0:T(8,128)S(1)}, f32[128,528]{1,0:T(8,128)S(1)}, f32[32,528]{1,0:T(8,128)S(1)}, f32[32,528]{1,0:T(8,128)S(1)}, f32[128,128]{1,0:T(...) custom-call(f32[4,32,528]{2,1,0:T(8,128)} %state.1, f32[4,32]{1,0:T(4,128)} %mass.1, f32[4,32]{1,0:T(4,128)} %inverse.1, ...), custom_call_target="tpu_custom_call" | custom-call | tf_op jit(solution)/shard_map/start/pallas_call | solution.py:261
  1.5 0.5 %collective-permute-start = (f32[32,528]{1,0:T(8,128)S(1)}, f32[32,528]{1,0:T(8,128)S(1)}, u32[]{:S(2)}, u32[]{:S(2)}) collective-permute-start(f32[32,528]{1,0:T(8,128)S(1)} %get-tuple-element.23), channel_id=1, source_target_pairs={{0,8},{8,16},{16,24},{24,0},{1,9},{9,17},{17,25},{25,1},{2,10},{10... | collective-permute-start | bytes 202760 | tf_op jit(solution)/shard_map/ppermute | solution.py:241
  2.0 2.0 %collective-permute-start.1 = (f32[32,528]{1,0:T(8,128)S(1)}, f32[32,528]{1,0:T(8,128)S(1)}, u32[]{:S(2)}, u32[]{:S(2)}) collective-permute-start(f32[32,528]{1,0:T(8,128)S(1)} %get-tuple-element.24), channel_id=1, source_target_pairs={{0,24},{8,0},{16,8},{24,16},{1,25},{9,1},{17,9},{25,17},{2,26},{10... | collective-permute-start | bytes 202760 | tf_op jit(solution)/shard_map/ppermute | solution.py:241
  4.0 2.1 %collective-permute-done.from_low = f32[32,528]{1,0:T(8,128)S(1)} collective-permute-done((f32[32,528]{1,0:T(8,128)S(1)}, f32[32,528]{1,0:T(8,128)S(1)}, u32[]{:S(2)}, u32[]{:S(2)}) %collective-permute-start) | collective-permute-done | bytes 67616 | tf_op jit(solution)/shard_map/ppermute | solution.py:241
  6.1 0.7 %collective-permute-done.1.from_high = f32[32,528]{1,0:T(8,128)S(1)} collective-permute-done((f32[32,528]{1,0:T(8,128)S(1)}, f32[32,528]{1,0:T(8,128)S(1)}, u32[]{:S(2)}, u32[]{:S(2)}) %collective-permute-start.1) | collective-permute-done | bytes 67616 | tf_op jit(solution)/shard_map/ppermute | solution.py:241
  6.8 0.3 %turn.1 = (f32[128,528]{1,0:T(8,128)S(1)}, f32[8,640]{1,0:T(8,128)S(1)}, f32[8,640]{1,0:T(8,128)S(1)}) custom-call(f32[128,528]{1,0:T(8,128)S(1)} %get-tuple-element.20.total, f32[128,128]{1,0:T(8,128)S(1)} %get-tuple-element.21.columns.masses, f32[128,128]{1,0:T(8,128)S(1)} %get-tuple-element.22.operator, f32[32,528]{1,0:T(8,128)S(1)} %collective-permute-done.from_low, ...), custom_call_target="tpu_custom_call" | custom-call | tf_op jit(solution)/shard_map/turn/pallas_call | solution.py:261
  7.1 1.6 %collective-permute-start.2 = (f32[8,640]{1,0:T(8,128)S(1)}, f32[8,640]{1,0:T(8,128)S(1)}, u32[]{:S(2)}, u32[]{:S(2)}) collective-permute-start(f32[8,640]{1,0:T(8,128)S(1)} %get-tuple-element.26), channel_id=1, source_target_pairs={{0,1},{1,2},{2,3},{3,4},{4,5},{5,6},{6,7},{7,0},{8,9},{9,10},{10,1... | collective-permute-start | bytes 61448 | tf_op jit(solution)/shard_map/ppermute | solution.py:241
  8.8 3.1 %collective-permute-start.3 = (f32[8,640]{1,0:T(8,128)S(1)}, f32[8,640]{1,0:T(8,128)S(1)}, u32[]{:S(2)}, u32[]{:S(2)}) collective-permute-start(f32[8,640]{1,0:T(8,128)S(1)} %get-tuple-element.27), channel_id=1, source_target_pairs={{0,7},{1,0},{2,1},{3,2},{4,3},{5,4},{6,5},{7,6},{8,15},{9,8},{10,9... | collective-permute-start | bytes 61448 | tf_op jit(solution)/shard_map/ppermute | solution.py:241
  11.8 1.6 %collective-permute-start.6 = (f32[144,128]{1,0:T(8,128)S(1)}, f32[144,128]{1,0:T(8,128)S(1)}, u32[]{:S(2)}, u32[]{:S(2)}) collective-permute-start(f32[144,128]{1,0:T(8,128)S(1)} %get-tuple-element.30.refs_0_), channel_id=1, source_target_pairs={{0,24},{8,0},{16,8},{24,16},{1,25},{9,1},{17,9},{25,17},{2,26},{10... | collective-permute-start | bytes 221192 | tf_op jit(solution)/shard_map/ppermute | solution.py:241
  13.4 1.4 %collective-permute-start.5 = (f32[144,128]{1,0:T(8,128)S(1)}, f32[144,128]{1,0:T(8,128)S(1)}, u32[]{:S(2)}, u32[]{:S(2)}) collective-permute-start(f32[144,128]{1,0:T(8,128)S(1)} %get-tuple-element.30.refs_0_), channel_id=1, source_target_pairs={{0,16},{8,24},{16,0},{24,8},{1,17},{9,25},{17,1},{25,9},{2,18},{10... | collective-permute-start | bytes 221192 | tf_op jit(solution)/shard_map/ppermute | solution.py:241
  14.8 0.0 collective-permute-start.4
  14.8 0.0 collective-permute-done.2.from_low
  14.8 0.0 collective-permute-done.3.from_high
  14.8 0.0 copy-start.1
  14.8 0.4 %second.1 = (f32[128,528]{1,0:T(8,128)S(1)}, f32[32,528]{1,0:T(8,128)S(1)}, f32[32,528]{1,0:T(8,128)S(1)}) custom-call(f32[128,528]{1,0:T(8,128)S(1)} %get-tuple-element.25.known, f32[128,128]{1,0:T(8,128)S(1)} %get-tuple-element.21.columns.masses, f32[128,128]{1,0:T(8,128)S(1)} %get-tuple-element.22.operator, f32[8,640]{1,0:T(8,128)S(1)} %collective-permute-done.2.from_low, ...), custom_call_target="tpu_custom_call" | custom-call | tf_op jit(solution)/shard_map/second/pallas_call | solution.py:261
  15.2 0.8 %collective-permute-start.7 = (f32[32,528]{1,0:T(8,128)S(1)}, f32[32,528]{1,0:T(8,128)S(1)}, u32[]{:S(2)}, u32[]{:S(2)}) collective-permute-start(f32[32,528]{1,0:T(8,128)S(1)} %get-tuple-element.31), channel_id=1, source_target_pairs={{0,8},{8,16},{16,24},{24,0},{1,9},{9,17},{17,25},{25,1},{2,10},{10... | collective-permute-start | bytes 202760 | tf_op jit(solution)/shard_map/ppermute | solution.py:241
  16.0 0.0 copy-start
  16.0 1.0 %collective-permute-start.8 = (f32[32,528]{1,0:T(8,128)S(1)}, f32[32,528]{1,0:T(8,128)S(1)}, u32[]{:S(2)}, u32[]{:S(2)}) collective-permute-start(f32[32,528]{1,0:T(8,128)S(1)} %get-tuple-element.32), channel_id=1, source_target_pairs={{0,24},{8,0},{16,8},{24,16},{1,25},{9,1},{17,9},{25,17},{2,26},{10... | collective-permute-start | bytes 202760 | tf_op jit(solution)/shard_map/ppermute | solution.py:241
  17.1 0.0 copy-done.1
  17.1 0.0 collective-permute-done.6.refs_3_
  17.1 1.4 %collective-permute-done.5.refs_2_ = f32[144,128]{1,0:T(8,128)S(1)} collective-permute-done((f32[144,128]{1,0:T(8,128)S(1)}, f32[144,128]{1,0:T(8,128)S(1)}, u32[]{:S(2)}, u32[]{:S(2)}) %collective-permute-start.5) | collective-permute-done | bytes 73760 | tf_op jit(solution)/shard_map/ppermute | solution.py:241
  18.5 0.5 %collective-permute-done.4.refs_1_ = f32[144,128]{1,0:T(8,128)S(1)} collective-permute-done((f32[144,128]{1,0:T(8,128)S(1)}, f32[144,128]{1,0:T(8,128)S(1)}, u32[]{:S(2)}, u32[]{:S(2)}) %collective-permute-start.4) | collective-permute-done | bytes 73760 | tf_op jit(solution)/shard_map/ppermute | solution.py:241
  18.9 0.0 copy-done
  18.9 0.9 %factors.1 = f32[288,128]{1,0:T(8,128)S(1)} custom-call(s32[4,32]{1,0:T(4,128)S(1)} %copy-done, f32[144,128]{1,0:T(8,128)S(1)} %get-tuple-element.30.refs_0_, f32[144,128]{1,0:T(8,128)S(1)} %collective-permute-done.4.refs_1_, f32[144,128]{1,0:T(8,128)S(1)} %collective-permute-done.5.refs_2_, f32[144,128]{1,0:T(8,128)S(1)} %collective-permute-done.6.refs_3_), custom_call_target="tpu_custom_call" | custom-call | tf_op jit(solution)/shard_map/factors/pallas_call | solution.py:261
  19.8 0.0 collective-permute-done.7.from_low
  19.8 0.0 collective-permute-done.8.from_high
  19.8 1.4 %third.1 = f32[4,32,528]{2,1,0:T(8,128)} custom-call(f32[4,32,528]{2,1,0:T(8,128)S(1)} %get-tuple-element.19.state, f32[1,528]{1,0:T(1,128)S(1)} %reshape.3.hyper, f32[128,528]{1,0:T(8,128)S(1)} %get-tuple-element.28.total, f32[128,128]{1,0:T(8,128)S(1)} %get-tuple-element.21.columns.masses, f32[288,128]{1,0:T(8,128)S(1)} %factors.1, ...), custom_call_target="tpu_custom_call" | custom-call | tf_op jit(solution)/shard_map/third/pallas_call | solution.py:261
  (1 shorter events, 0.0 us)
Async XLA Ops:
  1.5 4.6 %collective-permute-start = (f32[32,528]{1,0:T(8,128)S(1)}, f32[32,528]{1,0:T(8,128)S(1)}, u32[]{:S(2)}, u32[]{:S(2)}) collective-permute-start(f32[32,528]{1,0:T(8,128)S(1)} %get-tuple-element.23), channel_id=1, source_target_pairs={{0,8},{8,16},{16,24},{24,0},{1,9},{9,17},{17,25},{25,1},{2,10},{10... | collective-permute-start | bytes 202760 | tf_op jit(solution)/shard_map/ppermute | solution.py:241
  2.0 4.7 %collective-permute-start.1 = (f32[32,528]{1,0:T(8,128)S(1)}, f32[32,528]{1,0:T(8,128)S(1)}, u32[]{:S(2)}, u32[]{:S(2)}) collective-permute-start(f32[32,528]{1,0:T(8,128)S(1)} %get-tuple-element.24), channel_id=1, source_target_pairs={{0,24},{8,0},{16,8},{24,16},{1,25},{9,1},{17,9},{25,17},{2,26},{10... | collective-permute-start | bytes 202760 | tf_op jit(solution)/shard_map/ppermute | solution.py:241
  7.1 7.7 %collective-permute-start.2 = (f32[8,640]{1,0:T(8,128)S(1)}, f32[8,640]{1,0:T(8,128)S(1)}, u32[]{:S(2)}, u32[]{:S(2)}) collective-permute-start(f32[8,640]{1,0:T(8,128)S(1)} %get-tuple-element.26), channel_id=1, source_target_pairs={{0,1},{1,2},{2,3},{3,4},{4,5},{5,6},{6,7},{7,0},{8,9},{9,10},{10,1... | collective-permute-start | bytes 61448 | tf_op jit(solution)/shard_map/ppermute | solution.py:241
  8.8 6.0 %collective-permute-start.3 = (f32[8,640]{1,0:T(8,128)S(1)}, f32[8,640]{1,0:T(8,128)S(1)}, u32[]{:S(2)}, u32[]{:S(2)}) collective-permute-start(f32[8,640]{1,0:T(8,128)S(1)} %get-tuple-element.27), channel_id=1, source_target_pairs={{0,7},{1,0},{2,1},{3,2},{4,3},{5,4},{6,5},{7,6},{8,15},{9,8},{10,9... | collective-permute-start | bytes 61448 | tf_op jit(solution)/shard_map/ppermute | solution.py:241
  11.8 5.2 %collective-permute-start.6 = (f32[144,128]{1,0:T(8,128)S(1)}, f32[144,128]{1,0:T(8,128)S(1)}, u32[]{:S(2)}, u32[]{:S(2)}) collective-permute-start(f32[144,128]{1,0:T(8,128)S(1)} %get-tuple-element.30.refs_0_), channel_id=1, source_target_pairs={{0,24},{8,0},{16,8},{24,16},{1,25},{9,1},{17,9},{25,17},{2,26},{10... | collective-permute-start | bytes 221192 | tf_op jit(solution)/shard_map/ppermute | solution.py:241
  13.4 5.1 %collective-permute-start.5 = (f32[144,128]{1,0:T(8,128)S(1)}, f32[144,128]{1,0:T(8,128)S(1)}, u32[]{:S(2)}, u32[]{:S(2)}) collective-permute-start(f32[144,128]{1,0:T(8,128)S(1)} %get-tuple-element.30.refs_0_), channel_id=1, source_target_pairs={{0,16},{8,24},{16,0},{24,8},{1,17},{9,25},{17,1},{25,9},{2,18},{10... | collective-permute-start | bytes 221192 | tf_op jit(solution)/shard_map/ppermute | solution.py:241
  14.8 4.2 %collective-permute-start.4 = (f32[144,128]{1,0:T(8,128)S(1)}, f32[144,128]{1,0:T(8,128)S(1)}, u32[]{:S(2)}, u32[]{:S(2)}) collective-permute-start(f32[144,128]{1,0:T(8,128)S(1)} %get-tuple-element.30.refs_0_), channel_id=1, source_target_pairs={{0,8},{8,16},{16,24},{24,0},{1,9},{9,17},{17,25},{25,1},{2,10},{10... | collective-permute-start | bytes 221192 | tf_op jit(solution)/shard_map/ppermute | solution.py:241
  14.8 2.3 %copy-start.1 = (f32[528]{0:T(1024)S(1)}, f32[528]{0:T(1024)}, u32[]{:S(2)}) copy-start(f32[528]{0:T(1024)} %param.10) | copy-start | bytes 6340
  15.2 4.6 %collective-permute-start.7 = (f32[32,528]{1,0:T(8,128)S(1)}, f32[32,528]{1,0:T(8,128)S(1)}, u32[]{:S(2)}, u32[]{:S(2)}) collective-permute-start(f32[32,528]{1,0:T(8,128)S(1)} %get-tuple-element.31), channel_id=1, source_target_pairs={{0,8},{8,16},{16,24},{24,0},{1,9},{9,17},{17,25},{25,1},{2,10},{10... | collective-permute-start | bytes 202760 | tf_op jit(solution)/shard_map/ppermute | solution.py:241
  16.0 2.9 %copy-start = (s32[4,32]{1,0:T(4,128)S(1)}, s32[4,32]{1,0:T(4,128)}, u32[]{:S(2)}) copy-start(s32[4,32]{1,0:T(4,128)} %slots.1) | copy-start | bytes 1540
  16.0 3.8 %collective-permute-start.8 = (f32[32,528]{1,0:T(8,128)S(1)}, f32[32,528]{1,0:T(8,128)S(1)}, u32[]{:S(2)}, u32[]{:S(2)}) collective-permute-start(f32[32,528]{1,0:T(8,128)S(1)} %get-tuple-element.32), channel_id=1, source_target_pairs={{0,24},{8,0},{16,8},{24,16},{1,25},{9,1},{17,9},{25,17},{2,26},{10... | collective-permute-start | bytes 202760 | tf_op jit(solution)/shard_map/ppermute | solution.py:241

commit v4 on v3

--- a/solution.py
+++ b/solution.py
@@ -65,6 +65,16 @@
     return jnp.concatenate(parts, axis=0)
 
 
+def even(axis):
+    return lax.rem(lax.axis_index(axis), 2) == 0
+
+
+def x_rows(count, size_y):
+    near = jnp.where(even("gx"), count - size_y, 0)
+    far = count - size_y - near
+    return tuple(pl.ds(pl.multiple_of(start, size_y), size_y) for start in (near, far))
+
+
 def start_kernel(
     state,
     mass,
@@ -75,8 +85,8 @@
     tables,
     here,
     total,
-    x_low,
-    x_high,
+    x_near,
+    x_far,
     operator,
     columns,
     coefs,
@@ -106,8 +116,9 @@
     copies[3].wait()
     result = product(split(matrix), split(here[...].reshape(size_x * size_y, width)))
     total[...] = result
-    x_low[...] = result[:size_y]
-    x_high[...] = result[-size_y:]
+    near, far = x_rows(size_x * size_y, size_y)
+    x_near[...] = total[near]
+    x_far[...] = total[far]
     for copy in copies[4:]:
         copy.wait()
 
@@ -118,29 +129,36 @@
     )
 
 
-def turn_kernel(size_x, total, columns, operator, from_low, from_high, out, y_low, y_high):
-    size_y = from_low.shape[0]
+def turn_kernel(
+    size_x, total, columns, operator, from_far, from_near, out, y_near, y_far, y_low, y_high
+):
+    size_y = from_near.shape[0]
     width = total.shape[1]
+    near, far = x_rows(size_x * size_y, size_y)
     out[...] = total[...]
-    out[:size_y] += from_low[...]
-    out[-size_y:] += from_high[...]
+    out[near] += from_near[...]
+    out[far] += from_far[...]
     once = split(columns[:, 1:2] * out[...])
     for y, message in ((0, y_low), (size_y - 1, y_high)):
         rows = product(split(edge_rows(operator, y, size_x, size_y)), once)
         message[:size_x, :width] = edge_rows(out, y, size_x, size_y)
         message[size_x:, :width] = rows
         message[:size_x, width : width + 2] = edge_rows(columns, y, size_x, size_y)[:, :2]
+    y_near[...] = jnp.where(even("gy"), y_high[...], y_low[...])
+    y_far[...] = jnp.where(even("gy"), y_low[...], y_high[...])
 
 
 def second_kernel(
-    size_x, known, columns, operator, from_low, from_high, out, x_low, x_high, work
-):
-    size_y = x_low.shape[0]
+    size_x, known, columns, operator, from_far, from_near, out, x_near, x_far, work, low, high
+):
+    size_y = x_near.shape[0]
     width = known.shape[1]
     second = second_table()
     work[...] = known[...]
+    low[...] = jnp.where(even("gy"), from_far[...], from_near[...])
+    high[...] = jnp.where(even("gy"), from_near[...], from_far[...])
     beyond = []
-    for y, node, message in ((0, 3, from_low), (size_y - 1, 0, from_high)):
+    for y, node, message in ((0, 3, low), (size_y - 1, 0, high)):
         mass = message[:size_x, width : width + 1]
         inverse = message[:size_x, width + 1 : width + 2]
         theirs = inverse * edge_rows(known, y, size_x, size_y)
@@ -159,19 +177,21 @@
     for y, rows in zip((0, size_y - 1), beyond):
         for x in range(size_x):
             out[x * size_y + y : x * size_y + y + 1, :] += rows[x]
-    x_low[...] = out[:size_y]
-    x_high[...] = out[-size_y:]
+    near, far = x_rows(size_x * size_y, size_y)
+    x_near[...] = out[near]
+    x_far[...] = out[far]
 
 
 def third_kernel(
-    levels, state, hyper, total, masses, factors, from_low, from_high, out, work, turned, values
+    levels, state, hyper, total, masses, factors, from_far, from_near, out, work, turned, values
 ):
     columns, width = total.shape
     size_x, size_y, _ = state.shape
     variables = width // levels
+    near, far = x_rows(columns, size_y)
     work[...] = total[...]
-    work[:size_y] += from_low[...]
-    work[-size_y:] += from_high[...]
+    work[near] += from_near[...]
+    work[far] += from_far[...]
     twice = masses[:, 1:2] * work[...]
     turned[...] = (state[...].reshape(columns, width) - hyper[...] * twice).T
     scale, down, up, keep, flow, cloud = (
@@ -198,17 +218,15 @@
     out[...] = turned[...].T.reshape(out.shape)
 
 
-def factor_kernel(levels, shifts, slots, *refs):
+def factor_kernel(levels, owners, slots, *refs):
     pieces, factors = refs[:-1], refs[-1]
     span = pieces[0].shape[-1]
     size_x, size_y = slots.shape
     columns = size_x * size_y
-    peers, here = lax.axis_size("gx"), lax.axis_index("gx")
     picked = jnp.zeros((3 * levels, columns), jnp.float32)
     wanted = jnp.concatenate([slots[x : x + 1, :] for x in range(size_x)], axis=1)
-    for shift, piece in zip(shifts, pieces):
-        peer = lax.rem(here + peers - shift, peers)
-        entry = lax.broadcasted_iota(jnp.int32, (span, columns), 0) + peer * span
+    for owner, piece in zip(owners, pieces):
+        entry = lax.broadcasted_iota(jnp.int32, (span, columns), 0) + owner() * span
         choice = (entry == wanted).astype(jnp.float32).astype(jnp.bfloat16)
         rest = piece[...]
         for _ in range(3):
@@ -236,9 +254,15 @@
     cover[...] = covered
 
 
-def shifted(value, axis, step):
+def swapped(value, axis, partner):
+    return lax.ppermute(value, axis, [(i, partner(i)) for i in range(lax.axis_size(axis))])
+
+
+def exchanged(near, far, axis):
     size = lax.axis_size(axis)
-    return lax.ppermute(value, axis, [(i, (i + step) % size) for i in range(size)])
+    from_far = swapped(far, axis, lambda i: (i + (1 if i % 2 else -1)) % size)
+    from_near = swapped(near, axis, lambda i: i ^ 1)
+    return from_far, from_near
 
 
 def local(
@@ -269,7 +293,7 @@
         )(*operands)
 
     whole, line, edge = array(columns, width), array(size_y, width), array(2 * size_x, padded)
-    here, total, x_low, x_high, operator, masses, coefs = call(
+    here, total, x_near, x_far, operator, masses, coefs = call(
         start_kernel,
         "start",
         [
@@ -301,38 +325,38 @@
         ),
         spec=pl.BlockSpec(memory_space=pltpu.HBM),
     )
-    known, y_low, y_high = call(
+    known, y_near, y_far = call(
         functools.partial(turn_kernel, size_x),
         "turn",
         [whole, edge, edge],
-        [],
+        [scratch(2 * size_x, padded), scratch(2 * size_x, padded)],
         total,
         masses,
         operator,
-        shifted(x_high, "gx", 1),
-        shifted(x_low, "gx", -1),
-    )
-    total, x_low, x_high = call(
+        *exchanged(x_near, x_far, "gx"),
+    )
+    total, x_near, x_far = call(
         functools.partial(second_kernel, size_x),
         "second",
         [whole, line, line],
-        [scratch(columns, width)],
+        [scratch(columns, width), scratch(2 * size_x, padded), scratch(2 * size_x, padded)],
         known,
         masses,
         operator,
-        shifted(y_high, "gy", 1),
-        shifted(y_low, "gy", -1),
-    )
-    coefs, _ = lax.optimization_barrier((coefs, y_low))
-    shifts = range(lax.axis_size("gx"))
-    if len(shifts) <= 4:
-        pieces = [coefs] + [shifted(coefs, "gx", step) for step in shifts[1:]]
+        *exchanged(y_near, y_far, "gy"),
+    )
+    coefs, _ = lax.optimization_barrier((coefs, y_near))
+    peers = lax.axis_size("gx")
+    if peers == 4:
+        across = swapped(coefs, "gx", lambda i: i ^ 2)
+        pieces = [coefs, across]
+        pieces += [swapped(piece, "gx", lambda i: i ^ 1) for piece in pieces]
+        owners = [lambda bits=bits: lax.axis_index("gx") ^ bits for bits in (0, 2, 1, 3)]
     else:
-        gathered = lax.all_gather(coefs, "gx")
-        place = lax.axis_index("gx")
-        pieces = [gathered[(place - step) % len(shifts)] for step in shifts]
+        pieces = list(lax.all_gather(coefs, "gx"))
+        owners = [lambda peer=peer: peer for peer in range(peers)]
     (factors,) = call(
-        functools.partial(factor_kernel, levels, shifts),
+        functools.partial(factor_kernel, levels, owners),
         "factors",
         [array(6 * levels, columns)],
         [],
@@ -350,8 +374,7 @@
         total,
         masses,
         factors,
-        shifted(x_high, "gx", 1),
-        shifted(x_low, "gx", -1),
+        *exchanged(x_near, x_far, "gx"),
     )
     return result
 

time: 21.6 us -> 23.9 us (1.11)
  waiting for transfers between devices: 4.64 us -> 7.72 us
  starting transfers between devices: 12 us -> 11.4 us
    ppermute x9, waiting for transfers between devices: 4.64 us -> 7.72 us  [swapped(): lax.ppermute(value, axis, [(i, partner(i)) for i in range(lax.axis_size(a...]
    ppermute x9, starting transfers between devices: 12 us -> 11.4 us  [swapped(): lax.ppermute(value, axis, [(i, partner(i)) for i in range(lax.axis_size(a...]
  transfers between devices with their start and end apart: 9 -> 9, of which waited for: 4 -> 4; matrix products, arithmetic and copies ran while one was open for 0% -> 0% of each run, Pallas kernels for 6% -> 5%
where the time goes in v4:
time: 23.9 us; the launch traced here: 23.8 us
  starting transfers between devices  11.4 us (48%)
  waiting for transfers between devices  7.72 us (32%)
  Pallas kernels  4.58 us (19%)
    ppermute x9, starting transfers between devices, swapped(): lax.ppermute(value, axis, [(i, partner(i)) for i in range(lax.axis_size(a...  11.4 us
    ppermute x9, waiting for transfers between devices, swapped(): lax.ppermute(value, axis, [(i, partner(i)) for i in range(lax.axis_size(a...  7.72 us
    pallas_call x5, Pallas kernels, call(): pl.pallas_call(kernel, out_shape=outs, in_specs=[spec] * len(operands), o...  4.58 us
  transfers between devices with their start and end apart: 9, of which 4 were waited for; matrix products, arithmetic and copies ran while one was open for 0% of the time, Pallas kernels for 5%

profile of v4, /device:TPU:0, one launch (start us, length us, event | category | flops | bytes accessed | tf_op | source)
XLA Modules:
  0.0 23.8 jit_solution(8568171904169933071)
XLA Ops:
  0.0 1.5 %start.1 = (f32[4,32,528]{2,1,0:T(8,128)S(1)}, f32[128,528]{1,0:T(8,128)S(1)}, f32[32,528]{1,0:T(8,128)S(1)}, f32[32,528]{1,0:T(8,128)S(1)}, f32[128,128]{1,0:T(...) custom-call(f32[4,32,528]{2,1,0:T(8,128)} %state.1, f32[4,32]{1,0:T(4,128)} %mass.1, f32[4,32]{1,0:T(4,128)} %inverse.1, ...), custom_call_target="tpu_custom_call" | custom-call | tf_op jit(solution)/shard_map/start/pallas_call | solution.py:285
  1.5 2.4 %collective-permute-start = (f32[32,528]{1,0:T(8,128)S(1)}, f32[32,528]{1,0:T(8,128)S(1)}, u32[]{:S(2)}, u32[]{:S(2)}) collective-permute-start(f32[32,528]{1,0:T(8,128)S(1)} %get-tuple-element.23), channel_id=1, source_target_pairs={{0,24},{8,16},{16,8},{24,0},{1,25},{9,17},{17,9},{25,1},{2,26},{10... | collective-permute-start | bytes 202760 | tf_op jit(solution)/shard_map/ppermute | solution.py:258
  4.0 0.7 %collective-permute-start.1 = (f32[32,528]{1,0:T(8,128)S(1)}, f32[32,528]{1,0:T(8,128)S(1)}, u32[]{:S(2)}, u32[]{:S(2)}) collective-permute-start(f32[32,528]{1,0:T(8,128)S(1)} %get-tuple-element.24), channel_id=1, source_target_pairs={{0,8},{8,0},{16,24},{24,16},{1,9},{9,1},{17,25},{25,17},{2,10},{10... | collective-permute-start | bytes 202760 | tf_op jit(solution)/shard_map/ppermute | solution.py:258
  4.7 2.2 %collective-permute-done.from_far = f32[32,528]{1,0:T(8,128)S(1)} collective-permute-done((f32[32,528]{1,0:T(8,128)S(1)}, f32[32,528]{1,0:T(8,128)S(1)}, u32[]{:S(2)}, u32[]{:S(2)}) %collective-permute-start) | collective-permute-done | bytes 67616 | tf_op jit(solution)/shard_map/ppermute | solution.py:258
  6.8 0.0 collective-permute-done.1.from_near
  6.8 0.3 %turn.1 = (f32[128,528]{1,0:T(8,128)S(1)}, f32[8,640]{1,0:T(8,128)S(1)}, f32[8,640]{1,0:T(8,128)S(1)}) custom-call(f32[128,528]{1,0:T(8,128)S(1)} %get-tuple-element.20.total, f32[128,128]{1,0:T(8,128)S(1)} %get-tuple-element.21.columns.masses, f32[128,128]{1,0:T(8,128)S(1)} %get-tuple-element.22.operator, f32[32,528]{1,0:T(8,128)S(1)} %collective-permute-done.from_far, ...), custom_call_target="tpu_custom_call" | custom-call | tf_op jit(solution)/shard_map/turn/pallas_call | solution.py:285
  7.2 2.5 %collective-permute-start.4 = (f32[144,128]{1,0:T(8,128)S(1)}, f32[144,128]{1,0:T(8,128)S(1)}, u32[]{:S(2)}, u32[]{:S(2)}) collective-permute-start(f32[144,128]{1,0:T(8,128)S(1)} %get-tuple-element.30.refs_0_), channel_id=1, source_target_pairs={{0,16},{8,24},{16,0},{24,8},{1,17},{9,25},{17,1},{25,9},{2,18},{10... | collective-permute-start | bytes 221192 | tf_op jit(solution)/shard_map/ppermute | solution.py:258
  9.7 4.6 %collective-permute-start.2 = (f32[8,640]{1,0:T(8,128)S(1)}, f32[8,640]{1,0:T(8,128)S(1)}, u32[]{:S(2)}, u32[]{:S(2)}) collective-permute-start(f32[8,640]{1,0:T(8,128)S(1)} %get-tuple-element.26), channel_id=1, source_target_pairs={{0,7},{1,2},{2,1},{3,4},{4,3},{5,6},{6,5},{7,0},{8,15},{9,10},{10,... | collective-permute-start | bytes 61448 | tf_op jit(solution)/shard_map/ppermute | solution.py:258
  14.2 0.0 collective-permute-start.3
  14.2 0.0 collective-permute-start.5
  14.3 0.0 collective-permute-done.4.refs_1_
  14.3 0.5 %collective-permute-start.6 = (f32[144,128]{1,0:T(8,128)S(1)}, f32[144,128]{1,0:T(8,128)S(1)}, u32[]{:S(2)}, u32[]{:S(2)}) collective-permute-start(f32[144,128]{1,0:T(8,128)S(1)} %collective-permute-done.4.refs_1_), channel_id=1, source_target_pairs={{0,8},{8,0},{16,24},{24,16},{1,9},{9,1},{17,25},{25,17},{2,10},{10... | collective-permute-start | bytes 221192 | tf_op jit(solution)/shard_map/ppermute | solution.py:258
  14.8 1.4 %collective-permute-done.2.from_far = f32[8,640]{1,0:T(8,128)S(1)} collective-permute-done((f32[8,640]{1,0:T(8,128)S(1)}, f32[8,640]{1,0:T(8,128)S(1)}, u32[]{:S(2)}, u32[]{:S(2)}) %collective-permute-start.2) | collective-permute-done | bytes 20512 | tf_op jit(solution)/shard_map/ppermute | solution.py:258
  16.2 1.9 %collective-permute-done.3.from_near = f32[8,640]{1,0:T(8,128)S(1)} collective-permute-done((f32[8,640]{1,0:T(8,128)S(1)}, f32[8,640]{1,0:T(8,128)S(1)}, u32[]{:S(2)}, u32[]{:S(2)}) %collective-permute-start.3) | collective-permute-done | bytes 20512 | tf_op jit(solution)/shard_map/ppermute | solution.py:258
  18.0 0.0 copy-start.1
  18.0 0.4 %second.1 = (f32[128,528]{1,0:T(8,128)S(1)}, f32[32,528]{1,0:T(8,128)S(1)}, f32[32,528]{1,0:T(8,128)S(1)}) custom-call(f32[128,528]{1,0:T(8,128)S(1)} %get-tuple-element.25.known, f32[128,128]{1,0:T(8,128)S(1)} %get-tuple-element.21.columns.masses, f32[128,128]{1,0:T(8,128)S(1)} %get-tuple-element.22.operator, f32[8,640]{1,0:T(8,128)S(1)} %collective-permute-done.2.from_far, ...), custom_call_target="tpu_custom_call" | custom-call | tf_op jit(solution)/shard_map/second/pallas_call | solution.py:285
  18.4 0.1 collective-permute-start.7
  18.5 0.0 copy-start
  18.5 0.6 %collective-permute-start.8 = (f32[32,528]{1,0:T(8,128)S(1)}, f32[32,528]{1,0:T(8,128)S(1)}, u32[]{:S(2)}, u32[]{:S(2)}) collective-permute-start(f32[32,528]{1,0:T(8,128)S(1)} %get-tuple-element.32), channel_id=1, source_target_pairs={{0,8},{8,0},{16,24},{24,16},{1,9},{9,1},{17,25},{25,17},{2,10},{10... | collective-permute-start | bytes 202760 | tf_op jit(solution)/shard_map/ppermute | solution.py:258
  19.1 0.0 copy-done.1
  19.1 0.0 collective-permute-done.5.refs_2_
  19.1 0.0 collective-permute-done.6.refs_3_
  19.1 0.1 copy-done
  19.2 0.9 %factors.1 = f32[288,128]{1,0:T(8,128)S(1)} custom-call(s32[4,32]{1,0:T(4,128)S(1)} %copy-done, f32[144,128]{1,0:T(8,128)S(1)} %get-tuple-element.30.refs_0_, f32[144,128]{1,0:T(8,128)S(1)} %collective-permute-done.4.refs_1_, f32[144,128]{1,0:T(8,128)S(1)} %collective-permute-done.5.refs_2_, f32[144,128]{1,0:T(8,128)S(1)} %collective-permute-done.6.refs_3_), custom_call_target="tpu_custom_call" | custom-call | tf_op jit(solution)/shard_map/factors/pallas_call | solution.py:285
  20.1 2.3 %collective-permute-done.7.from_far = f32[32,528]{1,0:T(8,128)S(1)} collective-permute-done((f32[32,528]{1,0:T(8,128)S(1)}, f32[32,528]{1,0:T(8,128)S(1)}, u32[]{:S(2)}, u32[]{:S(2)}) %collective-permute-start.7) | collective-permute-done | bytes 67616 | tf_op jit(solution)/shard_map/ppermute | solution.py:258
  22.4 0.0 collective-permute-done.8.from_near
  22.4 1.4 %third.1 = f32[4,32,528]{2,1,0:T(8,128)} custom-call(f32[4,32,528]{2,1,0:T(8,128)S(1)} %get-tuple-element.19.state, f32[1,528]{1,0:T(1,128)S(1)} %reshape.3.hyper, f32[128,528]{1,0:T(8,128)S(1)} %get-tuple-element.28.total, f32[128,128]{1,0:T(8,128)S(1)} %get-tuple-element.21.columns.masses, f32[288,128]{1,0:T(8,128)S(1)} %factors.1, ...), custom_call_target="tpu_custom_call" | custom-call | tf_op jit(solution)/shard_map/third/pallas_call | solution.py:285
  (1 shorter events, 0.0 us)
Async XLA Ops:
  1.5 5.3 %collective-permute-start = (f32[32,528]{1,0:T(8,128)S(1)}, f32[32,528]{1,0:T(8,128)S(1)}, u32[]{:S(2)}, u32[]{:S(2)}) collective-permute-start(f32[32,528]{1,0:T(8,128)S(1)} %get-tuple-element.23), channel_id=1, source_target_pairs={{0,24},{8,16},{16,8},{24,0},{1,25},{9,17},{17,9},{25,1},{2,26},{10... | collective-permute-start | bytes 202760 | tf_op jit(solution)/shard_map/ppermute | solution.py:258
  4.0 2.8 %collective-permute-start.1 = (f32[32,528]{1,0:T(8,128)S(1)}, f32[32,528]{1,0:T(8,128)S(1)}, u32[]{:S(2)}, u32[]{:S(2)}) collective-permute-start(f32[32,528]{1,0:T(8,128)S(1)} %get-tuple-element.24), channel_id=1, source_target_pairs={{0,8},{8,0},{16,24},{24,16},{1,9},{9,1},{17,25},{25,17},{2,10},{10... | collective-permute-start | bytes 202760 | tf_op jit(solution)/shard_map/ppermute | solution.py:258
  7.2 7.1 %collective-permute-start.4 = (f32[144,128]{1,0:T(8,128)S(1)}, f32[144,128]{1,0:T(8,128)S(1)}, u32[]{:S(2)}, u32[]{:S(2)}) collective-permute-start(f32[144,128]{1,0:T(8,128)S(1)} %get-tuple-element.30.refs_0_), channel_id=1, source_target_pairs={{0,16},{8,24},{16,0},{24,8},{1,17},{9,25},{17,1},{25,9},{2,18},{10... | collective-permute-start | bytes 221192 | tf_op jit(solution)/shard_map/ppermute | solution.py:258
  9.7 6.5 %collective-permute-start.2 = (f32[8,640]{1,0:T(8,128)S(1)}, f32[8,640]{1,0:T(8,128)S(1)}, u32[]{:S(2)}, u32[]{:S(2)}) collective-permute-start(f32[8,640]{1,0:T(8,128)S(1)} %get-tuple-element.26), channel_id=1, source_target_pairs={{0,7},{1,2},{2,1},{3,4},{4,3},{5,6},{6,5},{7,0},{8,15},{9,10},{10,... | collective-permute-start | bytes 61448 | tf_op jit(solution)/shard_map/ppermute | solution.py:258
  14.2 3.8 %collective-permute-start.3 = (f32[8,640]{1,0:T(8,128)S(1)}, f32[8,640]{1,0:T(8,128)S(1)}, u32[]{:S(2)}, u32[]{:S(2)}) collective-permute-start(f32[8,640]{1,0:T(8,128)S(1)} %get-tuple-element.27), channel_id=1, source_target_pairs={{0,1},{1,0},{2,3},{3,2},{4,5},{5,4},{6,7},{7,6},{8,9},{9,8},{10,11... | collective-permute-start | bytes 61448 | tf_op jit(solution)/shard_map/ppermute | solution.py:258
  14.2 4.9 %collective-permute-start.5 = (f32[144,128]{1,0:T(8,128)S(1)}, f32[144,128]{1,0:T(8,128)S(1)}, u32[]{:S(2)}, u32[]{:S(2)}) collective-permute-start(f32[144,128]{1,0:T(8,128)S(1)} %get-tuple-element.30.refs_0_), channel_id=1, source_target_pairs={{0,8},{8,0},{16,24},{24,16},{1,9},{9,1},{17,25},{25,17},{2,10},{10... | collective-permute-start | bytes 221192 | tf_op jit(solution)/shard_map/ppermute | solution.py:258
  14.3 4.9 %collective-permute-start.6 = (f32[144,128]{1,0:T(8,128)S(1)}, f32[144,128]{1,0:T(8,128)S(1)}, u32[]{:S(2)}, u32[]{:S(2)}) collective-permute-start(f32[144,128]{1,0:T(8,128)S(1)} %collective-permute-done.4.refs_1_), channel_id=1, source_target_pairs={{0,8},{8,0},{16,24},{24,16},{1,9},{9,1},{17,25},{25,17},{2,10},{10... | collective-permute-start | bytes 221192 | tf_op jit(solution)/shard_map/ppermute | solution.py:258
  18.0 1.1 %copy-start.1 = (f32[528]{0:T(1024)S(1)}, f32[528]{0:T(1024)}, u32[]{:S(2)}) copy-start(f32[528]{0:T(1024)} %param.10) | copy-start | bytes 6340
  18.4 3.9 %collective-permute-start.7 = (f32[32,528]{1,0:T(8,128)S(1)}, f32[32,528]{1,0:T(8,128)S(1)}, u32[]{:S(2)}, u32[]{:S(2)}) collective-permute-start(f32[32,528]{1,0:T(8,128)S(1)} %get-tuple-element.31), channel_id=1, source_target_pairs={{0,24},{8,16},{16,8},{24,0},{1,25},{9,17},{17,9},{25,1},{2,26},{10... | collective-permute-start | bytes 202760 | tf_op jit(solution)/shard_map/ppermute | solution.py:258
  18.5 0.7 %copy-start = (s32[4,32]{1,0:T(4,128)S(1)}, s32[4,32]{1,0:T(4,128)}, u32[]{:S(2)}) copy-start(s32[4,32]{1,0:T(4,128)} %slots.1) | copy-start | bytes 1540
  18.5 3.8 %collective-permute-start.8 = (f32[32,528]{1,0:T(8,128)S(1)}, f32[32,528]{1,0:T(8,128)S(1)}, u32[]{:S(2)}, u32[]{:S(2)}) collective-permute-start(f32[32,528]{1,0:T(8,128)S(1)} %get-tuple-element.32), channel_id=1, source_target_pairs={{0,8},{8,0},{16,24},{24,16},{1,9},{9,1},{17,25},{25,17},{2,10},{10... | collective-permute-start | bytes 202760 | tf_op jit(solution)/shard_map/ppermute | solution.py:258

commit v5 on v4

--- a/solution.py
+++ b/solution.py
@@ -75,6 +75,24 @@
     return tuple(pl.ds(pl.multiple_of(start, size_y), size_y) for start in (near, far))
 
 
+COEF_ROWS = 32
+
+
+def write_coefs(message, start, coefs):
+    rows, lanes = coefs.shape
+    for i, first in enumerate(range(0, rows, COEF_ROWS)):
+        part = coefs[first : min(first + COEF_ROWS, rows)]
+        message[start : start + part.shape[0], i * lanes : (i + 1) * lanes] = part
+
+
+def read_coefs(message, start, rows, lanes):
+    parts = []
+    for i, first in enumerate(range(0, rows, COEF_ROWS)):
+        count = min(COEF_ROWS, rows - first)
+        parts.append(message[start : start + count, i * lanes : (i + 1) * lanes])
+    return jnp.concatenate(parts, axis=0)
+
+
 def start_kernel(
     state,
     mass,
@@ -87,12 +105,16 @@
     total,
     x_near,
     x_far,
+    y_near,
+    y_far,
     operator,
     columns,
     coefs,
     mass_here,
     inverse_here,
     tables_here,
+    low,
+    high,
     sems,
 ):
     size_x, size_y, width = state.shape
@@ -114,72 +136,104 @@
     matrix = own * tables_here[0] + to_column(mass_here[...], True) * tables_here[1]
     operator[...] = matrix
     copies[3].wait()
-    result = product(split(matrix), split(here[...].reshape(size_x * size_y, width)))
-    total[...] = result
+    total[...] = product(split(matrix), split(here[...].reshape(size_x * size_y, width)))
+    for first, message in ((0, low), (size_y - 4, high)):
+        for x in range(size_x):
+            for i in range(4):
+                row = x * size_y + first + i
+                place = i * size_x + x
+                message[place : place + 1, :width] = total[row : row + 1, :]
+                message[place : place + 1, width : width + 2] = columns[row : row + 1, :2]
+    y_near[...] = jnp.where(even("gy"), high[...], low[...])
+    y_far[...] = jnp.where(even("gy"), low[...], high[...])
     near, far = x_rows(size_x * size_y, size_y)
     x_near[...] = total[near]
-    x_far[...] = total[far]
+    x_far[:size_y, :width] = total[far]
     for copy in copies[4:]:
         copy.wait()
-
-
-def edge_rows(ref, y, size_x, size_y):
-    return jnp.concatenate(
-        [ref[x * size_y + y : x * size_y + y + 1, :] for x in range(size_x)], axis=0
-    )
-
-
-def turn_kernel(
-    size_x, total, columns, operator, from_far, from_near, out, y_near, y_far, y_low, y_high
+    if x_far.shape[0] > size_y:
+        write_coefs(x_far, size_y, coefs)
+
+
+def forward_kernel(size_x, width, from_far, from_near, x_near, x_far):
+    low = jnp.where(even("gy"), from_far[...], from_near[...])
+    high = jnp.where(even("gy"), from_near[...], from_far[...])
+
+    def edge(x):
+        rows = [
+            side[i * size_x + x : i * size_x + x + 1, :width]
+            for side in (low, high)
+            for i in range(4)
+        ]
+        return jnp.concatenate(rows, axis=0)
+
+    first, last = edge(0), edge(size_x - 1)
+    x_near[...] = jnp.where(even("gx"), last, first)
+    x_far[...] = jnp.where(even("gx"), first, last)
+
+
+def second_kernel(
+    size_x,
+    total,
+    columns,
+    operator,
+    coefs,
+    from_far,
+    from_near,
+    y_from_far,
+    y_from_near,
+    corner_far,
+    corner_near,
+    out,
+    x_near,
+    x_far,
+    work,
+    low,
+    high,
 ):
-    size_y = from_near.shape[0]
-    width = total.shape[1]
+    size_y, width = from_near.shape
+    second = second_table()
     near, far = x_rows(size_x * size_y, size_y)
-    out[...] = total[...]
-    out[near] += from_near[...]
-    out[far] += from_far[...]
-    once = split(columns[:, 1:2] * out[...])
-    for y, message in ((0, y_low), (size_y - 1, y_high)):
-        rows = product(split(edge_rows(operator, y, size_x, size_y)), once)
-        message[:size_x, :width] = edge_rows(out, y, size_x, size_y)
-        message[size_x:, :width] = rows
-        message[:size_x, width : width + 2] = edge_rows(columns, y, size_x, size_y)[:, :2]
-    y_near[...] = jnp.where(even("gy"), y_high[...], y_low[...])
-    y_far[...] = jnp.where(even("gy"), y_low[...], y_high[...])
-
-
-def second_kernel(
-    size_x, known, columns, operator, from_far, from_near, out, x_near, x_far, work, low, high
-):
-    size_y = x_near.shape[0]
-    width = known.shape[1]
-    second = second_table()
-    work[...] = known[...]
-    low[...] = jnp.where(even("gy"), from_far[...], from_near[...])
-    high[...] = jnp.where(even("gy"), from_near[...], from_far[...])
+    work[...] = total[...]
+    work[near] += from_near[...]
+    work[far] += from_far[:size_y, :width]
+    low[...] = jnp.where(even("gy"), y_from_far[...], y_from_near[...])
+    high[...] = jnp.where(even("gy"), y_from_near[...], y_from_far[...])
+    corners = (
+        (0, jnp.where(even("gx"), corner_far[...], corner_near[...])),
+        (size_x - 1, jnp.where(even("gx"), corner_near[...], corner_far[...])),
+    )
     beyond = []
-    for y, node, message in ((0, 3, low), (size_y - 1, 0, high)):
-        mass = message[:size_x, width : width + 1]
-        inverse = message[:size_x, width + 1 : width + 2]
-        theirs = inverse * edge_rows(known, y, size_x, size_y)
-        rows = []
+    for side, (message, y, line) in enumerate(((low, 0, 3), (high, size_y - 1, 0))):
+        for x, rows in corners:
+            for i in range(4):
+                place = i * size_x + x
+                message[place : place + 1, :width] += rows[side * 4 + i : side * 4 + i + 1]
         for x in range(size_x):
-            row = message[size_x + x : size_x + x + 1, :width]
-            line = sum(
-                float(second[x, i] + second[node, node] * (x == i)) * theirs[i : i + 1]
-                for i in range(size_x)
-            )
-            rows.append(row + mass[x : x + 1] * line)
-            work[x * size_y + y : x * size_y + y + 1, :] += message[x : x + 1, :width]
-        beyond.append(rows)
-    result = product(split(operator[...]), split(columns[:, 1:2] * work[...]))
-    out[...] = result
+            place, row = line * size_x + x, x * size_y + y
+            joined = message[place : place + 1, :width] + work[row : row + 1, :]
+            message[place : place + 1, :width] = joined
+            work[row : row + 1, :] = joined
+        once = message[:, width + 1 : width + 2] * message[:, :width]
+        lines = [once[i * size_x : (i + 1) * size_x] for i in range(4)]
+        value = sum(float(second[line, i]) * lines[i] for i in range(4))
+        place = lax.broadcasted_iota(jnp.int32, (size_x, 1), 0)
+        for i in range(size_x):
+            factor = jnp.zeros((size_x, 1), jnp.float32)
+            for x in range(size_x):
+                factor = jnp.where(place == x, float(second[x, i]), factor)
+            value = value + factor * lines[line][i : i + 1]
+        mass = message[line * size_x : (line + 1) * size_x, width : width + 1]
+        beyond.append(mass * value)
+    out[...] = product(split(operator[...]), split(columns[:, 1:2] * work[...]))
     for y, rows in zip((0, size_y - 1), beyond):
         for x in range(size_x):
-            out[x * size_y + y : x * size_y + y + 1, :] += rows[x]
-    near, far = x_rows(size_x * size_y, size_y)
-    x_near[...] = out[near]
+            out[x * size_y + y : x * size_y + y + 1, :] += rows[x : x + 1]
     x_far[...] = out[far]
+    x_near[:size_y, :width] = out[near]
+    if x_near.shape[0] > size_y:
+        write_coefs(x_near, size_y, coefs)
+        x_near[size_y + COEF_ROWS :, :] = from_far[size_y:, :]
 
 
 def third_kernel(
@@ -190,7 +244,7 @@
     variables = width // levels
     near, far = x_rows(columns, size_y)
     work[...] = total[...]
-    work[near] += from_near[...]
+    work[near] += from_near[:size_y, :width]
     work[far] += from_far[...]
     twice = masses[:, 1:2] * work[...]
     turned[...] = (state[...].reshape(columns, width) - hyper[...] * twice).T
@@ -218,17 +272,27 @@
     out[...] = turned[...].T.reshape(out.shape)
 
 
-def factor_kernel(levels, owners, slots, *refs):
-    pieces, factors = refs[:-1], refs[-1]
-    span = pieces[0].shape[-1]
+def factor_kernel(levels, span, slots, *refs):
+    rows = 3 * levels
     size_x, size_y = slots.shape
     columns = size_x * size_y
-    picked = jnp.zeros((3 * levels, columns), jnp.float32)
+    factors = refs[-1]
+    if len(refs) == 4:
+        own, from_far, from_near = refs[:3]
+        here = lax.axis_index("gx")
+        pieces = [
+            (here, own[...]),
+            (here ^ 3, read_coefs(from_far, size_y, rows, span)),
+            (here ^ 1, read_coefs(from_near, size_y, rows, span)),
+            (here ^ 2, read_coefs(from_near, size_y + COEF_ROWS, rows, span)),
+        ]
+    else:
+        pieces = [(peer, refs[0][peer]) for peer in range(refs[0].shape[0])]
+    picked = jnp.zeros((rows, columns), jnp.float32)
     wanted = jnp.concatenate([slots[x : x + 1, :] for x in range(size_x)], axis=1)
-    for owner, piece in zip(owners, pieces):
-        entry = lax.broadcasted_iota(jnp.int32, (span, columns), 0) + owner() * span
+    for owner, rest in pieces:
+        entry = lax.broadcasted_iota(jnp.int32, (span, columns), 0) + owner * span
         choice = (entry == wanted).astype(jnp.float32).astype(jnp.bfloat16)
-        rest = piece[...]
         for _ in range(3):
             part = rest.astype(jnp.bfloat16)
             rest = rest - part.astype(jnp.float32)
@@ -292,15 +356,20 @@
             name=name,
         )(*operands)
 
-    whole, line, edge = array(columns, width), array(size_y, width), array(2 * size_x, padded)
-    here, total, x_near, x_far, operator, masses, coefs = call(
+    riding = lax.axis_size("gx") == 4
+    extra = COEF_ROWS if riding else 0
+    whole, line = array(columns, width), array(size_y, width)
+    edge, corner = array(4 * size_x, padded), array(8, width)
+    here, total, x_near, x_far, y_near, y_far, operator, masses, coefs = call(
         start_kernel,
         "start",
         [
             array(size_x, size_y, width),
             whole,
             line,
-            line,
+            array(size_y + extra, padded),
+            edge,
+            edge,
             array(columns, columns),
             array(columns, 128),
             array(3 * levels, span),
@@ -309,6 +378,8 @@
             scratch(size_x, size_y),
             scratch(size_x, size_y),
             scratch(*tables.shape),
+            scratch(*edge.shape),
+            scratch(*edge.shape),
             pltpu.SemaphoreType.DMA((7,)),
         ],
         *(
@@ -325,45 +396,42 @@
         ),
         spec=pl.BlockSpec(memory_space=pltpu.HBM),
     )
-    known, y_near, y_far = call(
-        functools.partial(turn_kernel, size_x),
-        "turn",
-        [whole, edge, edge],
-        [scratch(2 * size_x, padded), scratch(2 * size_x, padded)],
+    from_y = exchanged(y_near, y_far, "gy")
+    from_x = exchanged(x_near, x_far, "gx")
+    corner_near, corner_far = call(
+        functools.partial(forward_kernel, size_x, width),
+        "forward",
+        [corner, corner],
+        [],
+        *from_y,
+    )
+    from_corner = exchanged(corner_near, corner_far, "gx")
+    total, x_near, x_far = call(
+        functools.partial(second_kernel, size_x),
+        "second",
+        [whole, array(size_y + 2 * extra, padded), line],
+        [scratch(columns, width), scratch(*edge.shape), scratch(*edge.shape)],
         total,
         masses,
         operator,
-        *exchanged(x_near, x_far, "gx"),
-    )
-    total, x_near, x_far = call(
-        functools.partial(second_kernel, size_x),
-        "second",
-        [whole, line, line],
-        [scratch(columns, width), scratch(2 * size_x, padded), scratch(2 * size_x, padded)],
-        known,
-        masses,
-        operator,
-        *exchanged(y_near, y_far, "gy"),
-    )
-    coefs, _ = lax.optimization_barrier((coefs, y_near))
-    peers = lax.axis_size("gx")
-    if peers == 4:
-        across = swapped(coefs, "gx", lambda i: i ^ 2)
-        pieces = [coefs, across]
-        pieces += [swapped(piece, "gx", lambda i: i ^ 1) for piece in pieces]
-        owners = [lambda bits=bits: lax.axis_index("gx") ^ bits for bits in (0, 2, 1, 3)]
+        coefs,
+        *from_x,
+        *from_y,
+        *from_corner,
+    )
+    last_x = exchanged(x_near, x_far, "gx")
+    if riding:
+        pieces = [coefs, from_x[0], last_x[1]]
     else:
-        pieces = list(lax.all_gather(coefs, "gx"))
-        owners = [lambda peer=peer: peer for peer in range(peers)]
+        pieces = [lax.all_gather(coefs, "gx")]
     (factors,) = call(
-        functools.partial(factor_kernel, levels, owners),
+        functools.partial(factor_kernel, levels, span),
         "factors",
         [array(6 * levels, columns)],
         [],
         span_slot,
         *pieces,
     )
-
     (result,) = call(
         functools.partial(third_kernel, levels),
         "third",
@@ -374,7 +442,7 @@
         total,
         masses,
         factors,
-        *exchanged(x_near, x_far, "gx"),
+        *last_x,
     )
     return result
 

time: 23.9 us -> 23 us (0.962)
  starting transfers between devices: 11.4 us -> 9.24 us
  waiting for transfers between devices: 7.72 us -> 9.13 us
  Pallas kernels: 4.58 us -> 4.34 us
    ppermute x9 -> x8, starting transfers between devices: 11.4 us -> 9.24 us  [swapped(): lax.ppermute(value, axis, [(i, partner(i)) for i in range(lax.axis_size(a...]
    ppermute x9 -> x8, waiting for transfers between devices: 7.72 us -> 9.13 us  [swapped(): lax.ppermute(value, axis, [(i, partner(i)) for i in range(lax.axis_size(a...]
  transfers between devices with their start and end apart: 9 -> 8, of which waited for: 4 -> 5; matrix products, arithmetic and copies ran while one was open for 0% -> 0% of each run, Pallas kernels for 5% -> 4%
where the time goes in v5:
time: 23 us; the launch traced here: 22.8 us
  starting transfers between devices  9.24 us (40%)
  waiting for transfers between devices  9.13 us (40%)
  Pallas kernels  4.34 us (19%)
    ppermute x8, starting transfers between devices, swapped(): lax.ppermute(value, axis, [(i, partner(i)) for i in range(lax.axis_size(a...  9.24 us
    ppermute x8, waiting for transfers between devices, swapped(): lax.ppermute(value, axis, [(i, partner(i)) for i in range(lax.axis_size(a...  9.13 us
    pallas_call x5, Pallas kernels, call(): pl.pallas_call(kernel, out_shape=outs, in_specs=[spec] * len(operands), o...  4.34 us
  transfers between devices with their start and end apart: 8, of which 5 were waited for; matrix products, arithmetic and copies ran while one was open for 0% of the time, Pallas kernels for 4%

profile of v5, /device:TPU:0, one launch (start us, length us, event | category | flops | bytes accessed | tf_op | source)
XLA Modules:
  0.0 22.8 jit_solution(10353423965666570694)
XLA Ops:
  0.0 1.6 %start.1 = (f32[4,32,528]{2,1,0:T(8,128)S(1)}, f32[128,528]{1,0:T(8,128)S(1)}, f32[32,528]{1,0:T(8,128)S(1)}, f32[64,640]{1,0:T(8,128)S(1)}, f32[16,640]{1,0:T(8...) custom-call(f32[4,32,528]{2,1,0:T(8,128)} %state.1, ...), custom_call_target="tpu_custom_call" | custom-call | tf_op jit(solution)/shard_map/start/pallas_call | solution.py:349
  1.6 2.4 %collective-permute-start = (f32[64,640]{1,0:T(8,128)S(1)}, f32[64,640]{1,0:T(8,128)S(1)}, u32[]{:S(2)}, u32[]{:S(2)}) collective-permute-start(f32[64,640]{1,0:T(8,128)S(1)} %get-tuple-element.24), channel_id=1, source_target_pairs={{0,24},{8,16},{16,8},{24,0},{1,25},{9,17},{17,9},{25,1},{2,26},{10... | collective-permute-start | bytes 491528 | tf_op jit(solution)/shard_map/ppermute | solution.py:322
  4.0 0.7 %collective-permute-start.1 = (f32[32,528]{1,0:T(8,128)S(1)}, f32[32,528]{1,0:T(8,128)S(1)}, u32[]{:S(2)}, u32[]{:S(2)}) collective-permute-start(f32[32,528]{1,0:T(8,128)S(1)} %get-tuple-element.25), channel_id=1, source_target_pairs={{0,8},{8,0},{16,24},{24,16},{1,9},{9,1},{17,25},{25,17},{2,10},{10... | collective-permute-start | bytes 202760 | tf_op jit(solution)/shard_map/ppermute | solution.py:322
  4.7 4.6 %collective-permute-start.2 = (f32[16,640]{1,0:T(8,128)S(1)}, f32[16,640]{1,0:T(8,128)S(1)}, u32[]{:S(2)}, u32[]{:S(2)}) collective-permute-start(f32[16,640]{1,0:T(8,128)S(1)} %get-tuple-element.26), channel_id=1, source_target_pairs={{0,7},{1,2},{2,1},{3,4},{4,3},{5,6},{6,5},{7,0},{8,15},{9,10},{10,... | collective-permute-start | bytes 122888 | tf_op jit(solution)/shard_map/ppermute | solution.py:322
  9.3 0.0 collective-permute-start.3
  9.3 2.1 %collective-permute-done.2.from_far.y_from_far = f32[16,640]{1,0:T(8,128)S(1)} collective-permute-done((f32[16,640]{1,0:T(8,128)S(1)}, f32[16,640]{1,0:T(8,128)S(1)}, u32[]{:S(2)}, u32[]{:S(2)}) %collective-permute-start.2) | collective-permute-done | bytes 40992 | tf_op jit(solution)/shard_map/ppermute | solution.py:322
  11.4 1.9 %collective-permute-done.3.from_near.y_from_near = f32[16,640]{1,0:T(8,128)S(1)} collective-permute-done((f32[16,640]{1,0:T(8,128)S(1)}, f32[16,640]{1,0:T(8,128)S(1)}, u32[]{:S(2)}, u32[]{:S(2)}) %collective-permute-start.3) | collective-permute-done | bytes 40992 | tf_op jit(solution)/shard_map/ppermute | solution.py:322
  13.3 0.1 collective-permute-start.4
  13.4 0.6 %collective-permute-start.5 = (f32[8,528]{1,0:T(8,128)S(1)}, f32[8,528]{1,0:T(8,128)S(1)}, u32[]{:S(2)}, u32[]{:S(2)}) collective-permute-start(f32[8,528]{1,0:T(8,128)S(1)} %get-tuple-element.29), channel_id=1, source_target_pairs={{0,8},{8,0},{16,24},{24,16},{1,9},{9,1},{17,25},{25,17},{2,10},{10... | collective-permute-start | bytes 50696 | tf_op jit(solution)/shard_map/ppermute | solution.py:322
  14.0 2.6 %collective-permute-done.4.corner_far = f32[8,528]{1,0:T(8,128)S(1)} collective-permute-done((f32[8,528]{1,0:T(8,128)S(1)}, f32[8,528]{1,0:T(8,128)S(1)}, u32[]{:S(2)}, u32[]{:S(2)}) %collective-permute-start.4) | collective-permute-done | bytes 16928 | tf_op jit(solution)/shard_map/ppermute | solution.py:322
  16.6 0.0 collective-permute-done.5.corner_near
  16.6 0.0 collective-permute-done.1.from_near
  16.6 0.0 collective-permute-done.from_far.refs_1_
  16.6 0.0 copy-start.1
  16.6 0.4 %second.1 = (f32[128,528]{1,0:T(8,128)S(1)}, f32[96,640]{1,0:T(8,128)S(1)}, f32[32,528]{1,0:T(8,128)S(1)}) custom-call(f32[128,528]{1,0:T(8,128)S(1)} %get-tuple-element.20.total, f32[128,128]{1,0:T(8,128)S(1)} %get-tuple-element.21.columns.masses, f32[128,128]{1,0:T(8,128)S(1)} %get-tuple-element.22.operator, ...), custom_call_target="tpu_custom_call" | custom-call | tf_op jit(solution)/shard_map/second/pallas_call | solution.py:349
  17.0 0.1 collective-permute-start.6
  17.1 0.0 copy-start
  17.1 0.8 %collective-permute-start.7 = (f32[32,528]{1,0:T(8,128)S(1)}, f32[32,528]{1,0:T(8,128)S(1)}, u32[]{:S(2)}, u32[]{:S(2)}) collective-permute-start(f32[32,528]{1,0:T(8,128)S(1)} %get-tuple-element.32), channel_id=1, source_target_pairs={{0,24},{8,16},{16,8},{24,0},{1,25},{9,17},{17,9},{25,1},{2,26},{10... | collective-permute-start | bytes 202760 | tf_op jit(solution)/shard_map/ppermute | solution.py:322
  17.9 0.0 copy-done.1
  17.9 0.7 %collective-permute-done.6.refs_2_.from_near = f32[96,640]{1,0:T(8,128)S(1)} collective-permute-done((f32[96,640]{1,0:T(8,128)S(1)}, f32[96,640]{1,0:T(8,128)S(1)}, u32[]{:S(2)}, u32[]{:S(2)}) %collective-permute-start.6) | collective-permute-done | bytes 245792 | tf_op jit(solution)/shard_map/ppermute | solution.py:322
  18.6 0.0 copy-done
  18.6 0.9 %factors.1 = f32[288,128]{1,0:T(8,128)S(1)} custom-call(s32[4,32]{1,0:T(4,128)S(1)} %copy-done, f32[144,128]{1,0:T(8,128)S(1)} %get-tuple-element.23.coefs.refs_0_, f32[64,640]{1,0:T(8,128)S(1)} %collective-permute-done.from_far.refs_1_, f32[96,640]{1,0:T(8,128)S(1)} %collective-permute-done.6.refs_2_.from_near), custom_call_target="tpu_custom_call" | custom-call | tf_op jit(solution)/shard_map/factors/pallas_call | solution.py:349
  19.5 1.9 %collective-permute-done.7.from_far = f32[32,528]{1,0:T(8,128)S(1)} collective-permute-done((f32[32,528]{1,0:T(8,128)S(1)}, f32[32,528]{1,0:T(8,128)S(1)}, u32[]{:S(2)}, u32[]{:S(2)}) %collective-permute-start.7) | collective-permute-done | bytes 67616 | tf_op jit(solution)/shard_map/ppermute | solution.py:322
  21.4 1.4 %third.1 = f32[4,32,528]{2,1,0:T(8,128)} custom-call(f32[4,32,528]{2,1,0:T(8,128)S(1)} %get-tuple-element.19.state, f32[1,528]{1,0:T(1,128)S(1)} %reshape.3.hyper, f32[128,528]{1,0:T(8,128)S(1)} %get-tuple-element.30.total, f32[128,128]{1,0:T(8,128)S(1)} %get-tuple-element.21.columns.masses, f32[288,128]{1,0:T(8,128)S(1)} %factors.1, ...), custom_call_target="tpu_custom_call" | custom-call | tf_op jit(solution)/shard_map/third/pallas_call | solution.py:349
  (2 shorter events, 0.0 us)
Async XLA Ops:
  1.6 15.0 %collective-permute-start = (f32[64,640]{1,0:T(8,128)S(1)}, f32[64,640]{1,0:T(8,128)S(1)}, u32[]{:S(2)}, u32[]{:S(2)}) collective-permute-start(f32[64,640]{1,0:T(8,128)S(1)} %get-tuple-element.24), channel_id=1, source_target_pairs={{0,24},{8,16},{16,8},{24,0},{1,25},{9,17},{17,9},{25,1},{2,26},{10... | collective-permute-start | bytes 491528 | tf_op jit(solution)/shard_map/ppermute | solution.py:322
  4.0 12.5 %collective-permute-start.1 = (f32[32,528]{1,0:T(8,128)S(1)}, f32[32,528]{1,0:T(8,128)S(1)}, u32[]{:S(2)}, u32[]{:S(2)}) collective-permute-start(f32[32,528]{1,0:T(8,128)S(1)} %get-tuple-element.25), channel_id=1, source_target_pairs={{0,8},{8,0},{16,24},{24,16},{1,9},{9,1},{17,25},{25,17},{2,10},{10... | collective-permute-start | bytes 202760 | tf_op jit(solution)/shard_map/ppermute | solution.py:322
  4.7 6.7 %collective-permute-start.2 = (f32[16,640]{1,0:T(8,128)S(1)}, f32[16,640]{1,0:T(8,128)S(1)}, u32[]{:S(2)}, u32[]{:S(2)}) collective-permute-start(f32[16,640]{1,0:T(8,128)S(1)} %get-tuple-element.26), channel_id=1, source_target_pairs={{0,7},{1,2},{2,1},{3,4},{4,3},{5,6},{6,5},{7,0},{8,15},{9,10},{10,... | collective-permute-start | bytes 122888 | tf_op jit(solution)/shard_map/ppermute | solution.py:322
  9.3 4.0 %collective-permute-start.3 = (f32[16,640]{1,0:T(8,128)S(1)}, f32[16,640]{1,0:T(8,128)S(1)}, u32[]{:S(2)}, u32[]{:S(2)}) collective-permute-start(f32[16,640]{1,0:T(8,128)S(1)} %get-tuple-element.27), channel_id=1, source_target_pairs={{0,1},{1,0},{2,3},{3,2},{4,5},{5,4},{6,7},{7,6},{8,9},{9,8},{10,11... | collective-permute-start | bytes 122888 | tf_op jit(solution)/shard_map/ppermute | solution.py:322
  13.3 3.3 %collective-permute-start.4 = (f32[8,528]{1,0:T(8,128)S(1)}, f32[8,528]{1,0:T(8,128)S(1)}, u32[]{:S(2)}, u32[]{:S(2)}) collective-permute-start(f32[8,528]{1,0:T(8,128)S(1)} %get-tuple-element.28), channel_id=1, source_target_pairs={{0,24},{8,16},{16,8},{24,0},{1,25},{9,17},{17,9},{25,1},{2,26},{10... | collective-permute-start | bytes 50696 | tf_op jit(solution)/shard_map/ppermute | solution.py:322
  13.4 3.2 %collective-permute-start.5 = (f32[8,528]{1,0:T(8,128)S(1)}, f32[8,528]{1,0:T(8,128)S(1)}, u32[]{:S(2)}, u32[]{:S(2)}) collective-permute-start(f32[8,528]{1,0:T(8,128)S(1)} %get-tuple-element.29), channel_id=1, source_target_pairs={{0,8},{8,0},{16,24},{24,16},{1,9},{9,1},{17,25},{25,17},{2,10},{10... | collective-permute-start | bytes 50696 | tf_op jit(solution)/shard_map/ppermute | solution.py:322
  16.6 1.3 %copy-start.1 = (f32[528]{0:T(1024)S(1)}, f32[528]{0:T(1024)}, u32[]{:S(2)}) copy-start(f32[528]{0:T(1024)} %param.10) | copy-start | bytes 6340
  17.0 1.6 %collective-permute-start.6 = (f32[96,640]{1,0:T(8,128)S(1)}, f32[96,640]{1,0:T(8,128)S(1)}, u32[]{:S(2)}, u32[]{:S(2)}) collective-permute-start(f32[96,640]{1,0:T(8,128)S(1)} %get-tuple-element.31), channel_id=1, source_target_pairs={{0,8},{8,0},{16,24},{24,16},{1,9},{9,1},{17,25},{25,17},{2,10},{10... | collective-permute-start | bytes 737288 | tf_op jit(solution)/shard_map/ppermute | solution.py:322
  17.1 1.5 %copy-start = (s32[4,32]{1,0:T(4,128)S(1)}, s32[4,32]{1,0:T(4,128)}, u32[]{:S(2)}) copy-start(s32[4,32]{1,0:T(4,128)} %slots.1) | copy-start | bytes 1540
  17.1 4.2 %collective-permute-start.7 = (f32[32,528]{1,0:T(8,128)S(1)}, f32[32,528]{1,0:T(8,128)S(1)}, u32[]{:S(2)}, u32[]{:S(2)}) collective-permute-start(f32[32,528]{1,0:T(8,128)S(1)} %get-tuple-element.32), channel_id=1, source_target_pairs={{0,24},{8,16},{16,8},{24,0},{1,25},{9,17},{17,9},{25,1},{2,26},{10... | collective-permute-start | bytes 202760 | tf_op jit(solution)/shard_map/ppermute | solution.py:322
